TPU v7x, 128 devices: a whole 4x4x4 slice. The times are simulated.
128 devices in a mesh: dp: 16 (over y, z), tensor: 8 (over x, core).
Axes of the slice: x: 4, y: 4, z: 4, core: 2. Of those that a mesh axis runs over, the one named last changes fastest.
Arguments:
- tokens: bfloat16 [80, 128, 3200], P('dp', 'tensor'), may hold values from -6 to 6
- norm_gain: float32 [3200], replicated, may hold values from 0.25 to 1.75
- fc1: bfloat16 [3200, 6400], P(None, 'tensor'), may hold values from -0.109375 to 0.109375
- fc2t: bfloat16 [3200, 6400], P(None, 'tensor'), may hold values from -0.078125 to 0.078125
- block_slot: int32 [80], replicated, may hold values from -1 to 31, as said below
- out_grad: bfloat16 [32, 128, 3200], P('dp', 'tensor'), may hold values from -6 to 6
Outputs:
- mixed: bfloat16 [32, 128, 3200], P('dp', 'tensor')
- tokens_grad: bfloat16 [80, 128, 3200], P('dp', 'tensor')
- fc1_grad: float32 [3200, 6400], P('dp', 'tensor')
- fc2t_grad: float32 [3200, 6400], P('dp', 'tensor')
- gain_grad: float32 [3200], replicated
Inputs may be any that keep to these rules, and one draw needn't show every extreme that they name: Home block b belongs to dp index b // 5 and balanced block s to dp index s // 2. block_slot is -1 for an empty home block; every balanced block is named by exactly one home block. Home block j of dp index r, when live, names a balanced block of dp index (r + j) mod the number of dp indices. Dp index 0 has all 5 of its home blocks live, and home block 1 of the last dp index is live.
All inputs are finite; a program needn't handle non-finite values.
Results may differ from a plain program's by a relative error of at most 0.0055.
Values may be sent and summed in bfloat16 or wider, within the bound.
A program may use at most 192 MiB of HBM per device.

v0:
```python
import jax
import jax.numpy as jnp
from jax import lax
from jax.sharding import PartitionSpec as P

ROW_DIMS = (((1,), (1,)), ((), ()))
COL_DIMS = (((0,), (0,)), ((), ()))


def shifted(shard, axis, by):
    devices = lax.axis_size(axis)
    return lax.ppermute(shard, axis, [(i, (i + by) % devices) for i in range(devices)])


def gelu_slope(value):
    normal_cdf = 0.5 * (1.0 + jax.scipy.special.erf(value * 0.7071067811865476))
    return normal_cdf + value * jnp.exp(-0.5 * value * value) * 0.3989422804014327


def route_tables(block_slot, home_count, slot_count):
    rank_count = lax.axis_size("dp")
    my_index = lax.axis_index("dp")
    slot_table = block_slot.reshape(rank_count, home_count)
    offsets = jnp.arange(home_count, dtype=jnp.int32)
    sender = (my_index - offsets) % rank_count
    entries = slot_table[sender, offsets]
    wanted = my_index * slot_count + jnp.arange(slot_count, dtype=jnp.int32)
    return (entries[None, :] == wanted[:, None]).astype(jnp.bfloat16)


def route_forward(blocks, take_pick):
    rank_count = lax.axis_size("dp")
    arrived = []
    for offset in range(blocks.shape[0]):
        stride = offset % rank_count
        if stride == 0:
            arrived.append(blocks[offset])
        else:
            arrived.append(shifted(blocks[offset], "dp", stride))
    stacked = jnp.stack(arrived)
    return jnp.einsum("sh,hrc->src", take_pick, stacked, preferred_element_type=jnp.float32).astype(
        jnp.bfloat16
    )


def route_back(blocks, take_pick):
    rank_count = lax.axis_size("dp")
    outgoing = jnp.einsum(
        "sh,src->hrc", take_pick, blocks, preferred_element_type=jnp.float32
    ).astype(jnp.bfloat16)
    returned = []
    for offset in range(outgoing.shape[0]):
        stride = offset % rank_count
        if stride == 0:
            returned.append(outgoing[offset])
        else:
            returned.append(shifted(outgoing[offset], "dp", -stride))
    return jnp.stack(returned)


def local(tokens, norm_gain, fc1, fc2t, block_slot, out_grad):
    home_count = tokens.shape[0]
    slot_count = out_grad.shape[0]
    take_pick = route_tables(block_slot, home_count, slot_count)
    grad_in = route_back(out_grad, take_pick)
    blocks, row_count, width = tokens.shape
    rows_flat = tokens.reshape(-1, width).astype(jnp.float32)
    inverse_rms = lax.rsqrt(jnp.mean(rows_flat * rows_flat, axis=-1, keepdims=True) + 1e-06)
    unit_rows = rows_flat * inverse_rms
    normed = (unit_rows * norm_gain).astype(jnp.bfloat16)
    normed_all = lax.all_gather(normed, "tensor", axis=0, tiled=True)
    pre_act = jnp.dot(normed_all, fc1, preferred_element_type=jnp.float32)
    hidden = jax.nn.gelu(pre_act, approximate=False).astype(jnp.bfloat16)
    part_rows = hidden
    branch = lax.psum_scatter(
        lax.dot_general(part_rows, fc2t, ROW_DIMS, preferred_element_type=jnp.float32),
        "tensor",
        scatter_dimension=0,
        tiled=True,
    )
    mixed_rows = (rows_flat + branch).astype(jnp.bfloat16).reshape(blocks, row_count, width)
    grad_flat = grad_in.reshape(-1, width)
    grad_all = lax.all_gather(grad_flat, "tensor", axis=0, tiled=True)
    hidden_grad = jnp.dot(grad_all, fc2t, preferred_element_type=jnp.float32)
    pre_grad = (hidden_grad * gelu_slope(pre_act)).astype(jnp.bfloat16)
    first = lax.dot_general(normed_all, pre_grad, COL_DIMS, preferred_element_type=jnp.float32)
    second = lax.dot_general(grad_all, hidden, COL_DIMS, preferred_element_type=jnp.float32)
    stacked = lax.psum_scatter(
        jnp.stack([first, second], axis=1), "dp", scatter_dimension=0, tiled=True
    )
    fc1_grad = stacked[:, 0]
    fc2t_grad = stacked[:, 1]
    part_rows = pre_grad
    normed_grad = lax.psum_scatter(
        lax.dot_general(part_rows, fc1, ROW_DIMS, preferred_element_type=jnp.float32),
        "tensor",
        scatter_dimension=0,
        tiled=True,
    )
    gain_grad = lax.psum(jnp.sum(normed_grad * unit_rows, axis=0), ("dp", "tensor"))
    scaled = normed_grad * norm_gain
    input_grad = grad_flat.astype(jnp.float32) + inverse_rms * (
        scaled - unit_rows * jnp.mean(scaled * unit_rows, axis=-1, keepdims=True)
    )
    input_grad = input_grad.astype(jnp.bfloat16).reshape(blocks, row_count, width)
    mixed = route_forward(mixed_rows, take_pick)
    return (mixed, input_grad, fc1_grad, fc2t_grad, gain_grad)


def solution(mesh):
    placed = (
        P("dp", "tensor", None),
        P(),
        P(None, "tensor"),
        P(None, "tensor"),
        P(),
        P("dp", "tensor", None),
    )
    return jax.shard_map(
        local,
        mesh=mesh,
        in_specs=placed,
        out_specs=(
            P("dp", "tensor", None),
            P("dp", "tensor", None),
            P("dp", "tensor"),
            P("dp", "tensor"),
            P(),
        ),
        check_vma=False,
    )
```

profile of v0, /device:TPU:0, one launch (start us, length us, event | category | flops | bytes accessed | tf_op | source)
XLA Modules:
  0.0 502.1 jit_solution(16303751393341207710)
XLA Ops:
  7.2 0.0 copy-start
  7.2 0.0 copy-start.6
  7.2 0.0 all-gather.3.cloned.1.call-start
  7.2 1.2 fusion.27
  8.5 0.1 rsqrt.12
  8.5 2.0 fusion.20
  10.6 0.0 all-gather.3.cloned.1.call-update
  10.6 0.0 all-gather.5.cloned.1.call-start
  10.7 0.1 reshape.108
  10.8 0.7 gather_fusion
  11.4 0.0 copy-done
  11.4 0.5 convolution_convert_fusion
  11.9 0.7 fusion.48
  12.7 6.6 %collective-permute-start.4 = (bf16[16,3200]{1,0:T(8,128)(2,1)S(1)}, bf16[16,3200]{1,0:T(8,128)(2,1)S(1)}, u32[]{:S(2)}, u32[]{:S(2)}) collective-permute-start(bf16[16,3200]{1,0:T(8,128)(2,1)S(1)} %bitcast.86), channel_id=1, source_target_pairs={{0,120},{8,0},{16,8},{24,16},{32,24},{40,32},{48,40},{56,48},{64,5... | collective-permute-start | bytes 307208 | tf_op jit(solution)/shard_map/ppermute | solution.py:12
  19.4 0.1 collective-permute-start.5
  19.5 1.5 collective-permute-start.6
  21.0 0.5 collective-permute-start.7
  21.5 1.1 collective-permute-done.4
  22.6 0.2 copy.59
  22.8 3.6 collective-permute-done.5
  26.5 0.2 copy.60
  26.6 0.8 collective-permute-done.6
  27.4 0.2 copy.61
  27.6 0.5 collective-permute-done.7
  28.1 0.2 copy.62
  28.2 1.7 stack.48
  30.0 0.8 copy.63
  30.8 0.0 all-gather.5.cloned.1.call-update
  30.9 0.3 reduce-scatter.5.cloned.1.call-start
  31.2 13.7 %all-gather.3.cloned.1.call-done = bf16[640,3200]{1,0:T(8,128)(2,1)} async-done(((bf16[80,3200]{1,0:T(8,128)(2,1)}), bf16[640,3200]{1,0:T(8,128)(2,1)}) %all-gather.3.cloned.1.call-update) | async-done | bytes 4096016 | tf_op jit(solution)/shard_map/all_gather | solution.py:71
  44.9 9.3 %fusion.50 = f32[640,800]{0,1:T(8,128)} fusion(bf16[640,3200]{1,0:T(8,128)(2,1)} %all-gather.3.cloned.1.call-done, bf16[3200,800]{0,1:T(8,128)(2,1)} %param.8), kind=kOutput, calls=%fused_computation.87 | convolution fusion | flops 3276800000 | bytes 11264000 | tf_op jit(solution)/shard_map/dot_general | solution.py:72
  54.2 24.6 %all-gather.5.cloned.1.call-done = bf16[640,3200]{1,0:T(8,128)(2,1)} async-done(((bf16[80,3200]{1,0:T(8,128)(2,1)}), bf16[640,3200]{1,0:T(8,128)(2,1)}) %all-gather.5.cloned.1.call-update) | async-done | bytes 4096016 | tf_op jit(solution)/shard_map/all_gather | solution.py:83
  78.8 8.7 %fusion.8 = bf16[640,800]{0,1:T(8,128)(2,1)S(1)} fusion(f32[640,800]{0,1:T(8,128)} %fusion.50, bf16[640,3200]{1,0:T(8,128)(2,1)} %all-gather.5.cloned.1.call-done, bf16[3200,800]{0,1:T(8,128)(2,1)} %param.9), kind=kOutput, calls=%fused_computation.16 | convolution fusion | flops 3281920000 | bytes 12288000 | tf_op jit(solution)/shard_map/dot_general | solution.py:84
  87.5 10.3 %fusion.51 = f32[640,3200]{1,0:T(8,128)} fusion(bf16[640,800]{0,1:T(8,128)(2,1)S(1)} %fusion.8, bf16[3200,800]{0,1:T(8,128)(2,1)} %param.8), kind=kOutput, calls=%fused_computation.88 | convolution fusion | flops 3276800000 | bytes 14336000 | tf_op jit(solution)/shard_map/dot_general | solution.py:95
  97.8 0.0 reduce-scatter.5.cloned.1.call-update
  97.8 0.6 reduce-scatter.3.cloned.1.call-start
  98.4 14.7 %fusion.46 = f32[640,3200]{1,0:T(8,128)} fusion(bf16[3200,800]{0,1:T(8,128)(2,1)} %param.9, f32[640,800]{0,1:T(8,128)} %fusion.50), kind=kOutput, calls=%fused_computation.84 | convolution fusion | flops 3310080000 | bytes 15360000 | tf_op jit(solution)/shard_map/dot_general | solution.py:76
  113.0 0.0 reduce-scatter.3.cloned.1.call-update
  113.1 0.2 all-reduce.3.cloned.1.call-start
  113.3 6.7 %convolution_bitcast_fusion.1 = f32[3200,1,800]{0,2,1:T(8,128)S(1)} fusion(bf16[640,800]{0,1:T(8,128)(2,1)S(1)} %fusion.8, bf16[640,3200]{1,0:T(8,128)(2,1)} %all-gather.3.cloned.1.call-done), kind=kOutput, calls=%fused_computation.3 | convolution fusion | flops 3276800000 | bytes 15360000 | tf_op jit(solution)/shard_map/dot_general | solution.py:86
  120.0 8.3 %convolution_bitcast_fusion = f32[3200,1,800]{0,2,1:T(8,128)S(1)} fusion(bf16[640,3200]{1,0:T(8,128)(2,1)S(1)} %copy-done.7, f32[640,800]{0,1:T(8,128)S(1)} %copy-done.9), kind=kOutput, calls=%fused_computation.2 | convolution fusion | flops 3310080000 | bytes 16384000 | tf_op jit(solution)/shard_map/dot_general | solution.py:87
  128.3 7.5 %pad_maximum_fusion = f32[3200,2,800]{0,2,1:T(8,128)} fusion(f32[3200,1,800]{0,2,1:T(8,128)S(1)} %convolution_bitcast_fusion, f32[3200,1,800]{0,2,1:T(8,128)S(1)} %convolution_bitcast_fusion.1), kind=kLoop, calls=%fused_computation.1 | loop fusion | flops 5120000 | bytes 40960000 | tf_op jit(solution)/shard_map/stack | solution.py:89
  135.8 36.3 %copy.64 = f32[3200,2,800]{2,1,0:T(2,128)} copy(f32[3200,2,800]{0,2,1:T(8,128)} %pad_maximum_fusion) | data formatting | bytes 40960000 | tf_op jit(solution)/shard_map/stack | solution.py:89
  172.1 0.0 all-reduce.3.cloned.1.call-update
  172.1 0.6 copy-done.8
  172.7 0.6 dynamic-slice
  173.9 0.0 reduce-scatter.5.cloned.1.call-done
  174.0 1.7 fusion.26
  175.7 27.2 %reduce-scatter.3.cloned.1.call-done = f32[80,3200]{1,0:T(8,128)} async-done(((f32[640,3200]{1,0:T(8,128)}), f32[80,3200]{1,0:T(8,128)}) %reduce-scatter.3.cloned.1.call-update) | async-done | bytes 1024016 | tf_op jit(solution)/shard_map/reduce_scatter | solution.py:75
  202.9 2.4 fusion.25
  205.4 1.6 collective-permute-start
  207.0 2.9 collective-permute-start.1
  209.9 2.3 collective-permute-start.2
  212.3 1.5 collective-permute-start.3
  213.7 66.5 %psum.7 = f32[3200]{0:T(1024)} all-reduce(f32[3200]{0:T(1024)S(1)} %get-tuple-element.40), channel_id=1, replica_groups=mesh['dp'=16,'tensor'=8] {'dp','tensor'}, use_global_device_ids=true, to_apply=%region_6.7 | all-reduce | flops 3200 | bytes 25600 | tf_op jit(solution)/shard_map/psum | solution.py:100
  280.2 0.0 collective-permute-done
  280.2 0.0 collective-permute-done.1
  280.2 0.0 collective-permute-done.2
  280.3 0.0 collective-permute-done.3
  280.3 0.4 convolution_convert_fusion.1
  280.7 0.7 copy.65
  281.4 209.6 %all-reduce.3.cloned.1.call-done = f32[3200,2,800]{2,1,0:T(2,128)} async-done(((f32[3200,2,800]{2,1,0:T(2,128)}), f32[3200,2,800]{2,1,0:T(2,128)}) %all-reduce.3.cloned.1.call-update) | async-done | bytes 20480016
  491.1 3.1 constant_dynamic-slice_fusion.1
  494.2 1.2 copy_bitcast_fusion
  (30 shorter events, 0.2 us)
Async XLA Ops:
  7.2 4.3 copy-start
  7.2 3.5 copy-start.6
  7.2 37.7 %all-gather.3.cloned.1.call-start = ((), (), s32[]{:S(2)}) async-start(), calls=%async_computation.2 | async-start | bytes 4608000 | tf_op jit(solution)/shard_map/all_gather | solution.py:71
  10.6 68.2 %all-gather.5.cloned.1.call-start = ((), (), s32[]{:S(2)}) async-start(), calls=%async_computation.4 | async-start | bytes 4608000 | tf_op jit(solution)/shard_map/all_gather | solution.py:83
  12.7 9.9 %collective-permute-start.4 = (bf16[16,3200]{1,0:T(8,128)(2,1)S(1)}, bf16[16,3200]{1,0:T(8,128)(2,1)S(1)}, u32[]{:S(2)}, u32[]{:S(2)}) collective-permute-start(bf16[16,3200]{1,0:T(8,128)(2,1)S(1)} %bitcast.86), channel_id=1, source_target_pairs={{0,120},{8,0},{16,8},{24,16},{32,24},{40,32},{48,40},{56,48},{64,5... | collective-permute-start | bytes 307208 | tf_op jit(solution)/shard_map/ppermute | solution.py:12
  19.4 7.1 %collective-permute-start.5 = (bf16[16,3200]{1,0:T(8,128)(2,1)S(1)}, bf16[16,3200]{1,0:T(8,128)(2,1)S(1)}, u32[]{:S(2)}, u32[]{:S(2)}) collective-permute-start(bf16[16,3200]{1,0:T(8,128)(2,1)S(1)} %bitcast.88), channel_id=1, source_target_pairs={{0,112},{8,120},{16,0},{24,8},{32,16},{40,24},{48,32},{56,40},{64,... | collective-permute-start | bytes 307208 | tf_op jit(solution)/shard_map/ppermute | solution.py:12
  19.5 8.0 %collective-permute-start.6 = (bf16[16,3200]{1,0:T(8,128)(2,1)S(1)}, bf16[16,3200]{1,0:T(8,128)(2,1)S(1)}, u32[]{:S(2)}, u32[]{:S(2)}) collective-permute-start(bf16[16,3200]{1,0:T(8,128)(2,1)S(1)} %bitcast.90), channel_id=1, source_target_pairs={{0,104},{8,112},{16,120},{24,0},{32,8},{40,16},{48,24},{56,32},{64... | collective-permute-start | bytes 307208 | tf_op jit(solution)/shard_map/ppermute | solution.py:12
  21.0 7.1 %collective-permute-start.7 = (bf16[16,3200]{1,0:T(8,128)(2,1)S(1)}, bf16[16,3200]{1,0:T(8,128)(2,1)S(1)}, u32[]{:S(2)}, u32[]{:S(2)}) collective-permute-start(bf16[16,3200]{1,0:T(8,128)(2,1)S(1)} %bitcast.92), channel_id=1, source_target_pairs={{0,96},{8,104},{16,112},{24,120},{32,0},{40,8},{48,16},{56,24},{64... | collective-permute-start | bytes 307208 | tf_op jit(solution)/shard_map/ppermute | solution.py:12
  30.9 143.1 %reduce-scatter.5.cloned.1.call-start = ((), (), s32[]{:S(2)}) async-start(), calls=%async_computation.5 | async-start | bytes 9216000 | tf_op jit(solution)/shard_map/reduce_scatter | solution.py:94
  97.8 105.1 %reduce-scatter.3.cloned.1.call-start = ((), (), s32[]{:S(2)}) async-start(), calls=%async_computation.3 | async-start | bytes 9216000 | tf_op jit(solution)/shard_map/reduce_scatter | solution.py:75
  113.1 378.0 %all-reduce.3.cloned.1.call-start = ((), (), s32[]{:S(2)}) async-start(), calls=%async_computation.6 | async-start | bytes 45875200
  113.3 6.7 %copy-start.7 = (bf16[640,3200]{1,0:T(8,128)(2,1)S(1)}, bf16[640,3200]{1,0:T(8,128)(2,1)}, u32[]{:S(2)}) copy-start(bf16[640,3200]{1,0:T(8,128)(2,1)} %all-gather.5.cloned.1.call-done) | copy-start | bytes 12288004
  113.3 6.7 %copy-start.9 = (f32[640,800]{0,1:T(8,128)S(1)}, f32[640,800]{0,1:T(8,128)}, u32[]{:S(2)}) copy-start(f32[640,800]{0,1:T(8,128)} %fusion.50) | copy-start | bytes 6144004
  172.0 0.7 copy-start.8
  172.0 1.9 copy-start.2
  172.0 1.9 copy-start.5
  172.0 30.9 %copy-start.3 = (bf16[5,16,3200]{2,1,0:T(8,128)(2,1)S(1)}, bf16[5,16,3200]{2,1,0:T(8,128)(2,1)}, u32[]{:S(2)}) copy-start(bf16[5,16,3200]{2,1,0:T(8,128)(2,1)} %copy.63) | copy-start | bytes 1536004
  174.0 28.9 %copy-start.4 = (f32[80,3200]{1,0:T(8,128)S(1)}, f32[80,3200]{1,0:T(8,128)}, u32[]{:S(2)}) copy-start(f32[80,3200]{1,0:T(8,128)} %reduce-scatter.5.cloned.1.call-done) | copy-start | bytes 3072004
  205.4 74.8 %collective-permute-start = (bf16[16,3200]{1,0:T(8,128)(2,1)S(1)}, bf16[16,3200]{1,0:T(8,128)(2,1)S(1)}, u32[]{:S(2)}, u32[]{:S(2)}) collective-permute-start(bf16[16,3200]{1,0:T(8,128)(2,1)S(1)} %get-tuple-element.54), channel_id=1, source_target_pairs={{0,8},{8,16},{16,24},{24,32},{32,40},{40,48},{48,56},{56,64},{64,7... | collective-permute-start | bytes 307208 | tf_op jit(solution)/shard_map/ppermute | solution.py:12
  207.0 73.2 %collective-permute-start.1 = (bf16[16,3200]{1,0:T(8,128)(2,1)S(1)}, bf16[16,3200]{1,0:T(8,128)(2,1)S(1)}, u32[]{:S(2)}, u32[]{:S(2)}) collective-permute-start(bf16[16,3200]{1,0:T(8,128)(2,1)S(1)} %get-tuple-element.53), channel_id=1, source_target_pairs={{0,16},{8,24},{16,32},{24,40},{32,48},{40,56},{48,64},{56,72},{64,... | collective-permute-start | bytes 307208 | tf_op jit(solution)/shard_map/ppermute | solution.py:12
  209.9 70.3 %collective-permute-start.2 = (bf16[16,3200]{1,0:T(8,128)(2,1)S(1)}, bf16[16,3200]{1,0:T(8,128)(2,1)S(1)}, u32[]{:S(2)}, u32[]{:S(2)}) collective-permute-start(bf16[16,3200]{1,0:T(8,128)(2,1)S(1)} %get-tuple-element.52), channel_id=1, source_target_pairs={{0,24},{8,32},{16,40},{24,48},{32,56},{40,64},{48,72},{56,80},{64,... | collective-permute-start | bytes 307208 | tf_op jit(solution)/shard_map/ppermute | solution.py:12
  212.3 68.0 %collective-permute-start.3 = (bf16[16,3200]{1,0:T(8,128)(2,1)S(1)}, bf16[16,3200]{1,0:T(8,128)(2,1)S(1)}, u32[]{:S(2)}, u32[]{:S(2)}) collective-permute-start(bf16[16,3200]{1,0:T(8,128)(2,1)S(1)} %get-tuple-element.51), channel_id=1, source_target_pairs={{0,32},{8,40},{16,48},{24,56},{32,64},{40,72},{48,80},{56,88},{64,... | collective-permute-start | bytes 307208 | tf_op jit(solution)/shard_map/ppermute | solution.py:12
  491.1 4.3 copy-start.1
Sparse Core Ops, SparseCore 0:
  10.7 34.1 all-gather.2
  47.1 31.6 all-gather.4
  97.9 51.4 reduce-scatter.4
  151.8 51.0 reduce-scatter.2
  206.5 284.5 all-reduce.2
where the time goes:
time: 508 us; the launch traced here: 502 us
  waiting for transfers between devices  281 us (55%)
  blocking collectives  66.5 us (13%)
  matrix products  58.8 us (12%)
  local copies, waits for them, and re-layouts  47.4 us (9%)
  starting transfers between devices  18.2 us (4%)
  other arithmetic  14.9 us (3%)
  between operations  14.9 us (3%)
    unnamed x6, waiting for transfers between devices  210 us
    psum x1, blocking collectives, local(): lax.psum(jnp.sum(normed_grad * unit_rows, axis=0), ('dp', 'tensor'))  66.5 us
    another operation x1, local copies, waits for them, and re-layouts, local(): jnp.stack([first, second], axis=1)  36.3 us
    reduce_scatter x1, waiting for transfers between devices, local(): lax.psum_scatter(lax.dot_general(part_rows, fc2t, ROW_DIMS, preferred_ele...  27.2 us
    all_gather x1, waiting for transfers between devices, local(): grad_all = lax.all_gather(grad_flat, 'tensor', axis=0, tiled=True)  24.6 us
    ppermute x8, starting transfers between devices, shifted(): lax.ppermute(shard, axis, [(i, (i + by) % devices) for i in range(devices)])  17 us
    dot_general x1, matrix products, local(): lax.dot_general(part_rows, fc2t, ROW_DIMS, preferred_element_type=jnp.flo...  14.7 us
    all_gather x1, waiting for transfers between devices, local(): normed_all = lax.all_gather(normed, 'tensor', axis=0, tiled=True)  13.7 us
  transfers between devices with their start and end apart: 13, of which 8 were waited for; matrix products, arithmetic and copies ran while one was open for 19% of the time, Pallas kernels for 0%

commit v1 on v0

v1 whole, which is shorter than its diff:
```python
import functools

import jax
import jax.numpy as jnp
from jax import lax
from jax.experimental import pallas as pl
from jax.experimental.pallas import tpu as pltpu
from jax.sharding import PartitionSpec as P

MESH = pl.DeviceIdType.MESH
ROW_DIMS = (((1,), (1,)), ((), ()))
RING = 4
F32 = jnp.float32
BF16 = jnp.bfloat16


def round_up(value, unit):
    return (value + unit - 1) // unit * unit


def chunk_of(width, limit):
    tiles = width // 128
    best = 1
    for count in range(1, tiles + 1):
        if tiles % count == 0 and count * 128 <= limit:
            best = count
    return best * 128


class Sizes:
    def __init__(self, tokens, fc1, out_grad):
        self.homes, self.block_rows, self.width = tokens
        self.units = fc1[1]
        self.slots = out_grad[0]
        self.own = self.slots * self.block_rows
        self.rows = 2 * RING * self.own
        self.owned = self.width // (RING * RING)
        self.owned_pad = round_up(self.owned, 16)
        self.window = round_up(self.owned + 127, 128)
        self.last_tile = (self.width - self.window) // 128
        self.chunk = chunk_of(self.width, 640)


def kernel(
    sz,
    copies,
    slot_ref,
    gain_ref,
    tokens_ref,
    fc1_hbm,
    fc2_hbm,
    grad_hbm,
    mixed_ref,
    tgrad_ref,
    fc1_grad_ref,
    fc2_grad_ref,
    gain_grad_ref,
    fc1_ref,
    fc2_ref,
    arrived,
    row_in,
    inv_ref,
    grad_all,
    norm_all,
    grad_t,
    norm_t,
    grad_tg,
    norm_tg,
    hid_g,
    pre_g,
    pre_act,
    hid_grad,
    row_sum,
    sib_out,
    sib_in,
    rs_out,
    rs_in,
    wg_sum,
    wg_out,
    wg_in,
    back_out,
    input_grad,
    gain_sib,
    gain_x,
    gain_y,
    gain_z,
    local_sems,
    send_sems,
    recv_sems,
):
    dp = lax.axis_index("dp")
    t = lax.axis_index("tensor")
    y, z = dp // RING, dp % RING
    x, c = t // 2, t % 2
    ranks = RING * RING
    own, width, units = sz.own, sz.width, sz.units
    half = own // 2

    def on_dp(k):
        return ((dp + k + ranks) % ranks, t)

    def on_x(k):
        return (dp, ((x + k + RING) % RING) * 2 + c)

    def on_y(k):
        return (((y + k + RING) % RING) * RING + z, t)

    def on_z(k):
        return (y * RING + (z + k + RING) % RING, t)

    sibling = (dp, t + 1 - 2 * c)

    started = []

    def send(src, dst, device):
        index = len(started)
        made = pltpu.make_async_remote_copy(
            src_ref=src,
            dst_ref=dst,
            send_sem=send_sems.at[index],
            recv_sem=recv_sems.at[index],
            device_id=device,
            device_id_type=MESH,
        )
        made.start()
        started.append(made)
        return made

    def at(base, k):
        return (base + k + RING) % RING

    my_rows = pl.ds(pl.multiple_of(t * own, own), own)
    load_grad = pltpu.make_async_copy(grad_hbm, grad_all.at[my_rows], local_sems.at[0])
    load_fc2 = pltpu.make_async_copy(fc2_hbm, fc2_ref, local_sems.at[1])
    load_fc1 = pltpu.make_async_copy(fc1_hbm, fc1_ref, local_sems.at[2])
    load_grad.start()
    load_fc2.start()
    load_fc1.start()

    partners = [on_dp(k) for k in range(1, sz.homes)]
    partners += [on_dp(-k) for k in range(1, sz.homes)]
    partners += [on_y(k) for k in (1, -1, 2)]
    partners += [on_z(k) for k in (1, -1, 2)]
    partners += [on_x(k) for k in (1, -1, 2)]
    partners += [sibling]
    barrier = pltpu.get_barrier_semaphore()
    for device in partners:
        pl.semaphore_signal(barrier, inc=1, device_id=device, device_id_type=MESH)
    pl.semaphore_wait(barrier, len(partners))

    routed = [
        send(tokens_ref.at[j], arrived.at[j - 1], on_dp(j)) for j in range(1, sz.homes)
    ]

    class RowGather:
        def __init__(self, buf):
            self.buf = buf

        def part(self, k, core, lo, count):
            place = (at(x, k) * 2 + core) * own + lo
            return self.buf.at[pl.ds(pl.multiple_of(place, 16), count)]

        def start(self):
            mine = self.part(0, c, 0, own)
            self.right = send(mine, mine, on_x(1))
            self.left = send(mine, mine, on_x(-1))
            self.shared = [send(mine, mine, sibling)]

        def forward(self):
            self.right.wait_recv()
            low = self.part(-1, c, 0, half)
            self.right2 = send(low, low, on_x(1))
            whole = self.part(-1, c, 0, own)
            self.shared.append(send(whole, whole, sibling))
            self.left.wait_recv()
            high = self.part(1, c, half, own - half)
            self.left2 = send(high, high, on_x(-1))
            whole = self.part(1, c, 0, own)
            self.shared.append(send(whole, whole, sibling))

        def finish(self):
            self.right2.wait_recv()
            low = self.part(2, c, 0, half)
            self.shared.append(send(low, low, sibling))
            self.left2.wait_recv()
            high = self.part(2, c, half, own - half)
            self.shared.append(send(high, high, sibling))
            for made in self.shared:
                made.wait_recv()

    class RingGather:
        def __init__(self, buf, me, on_axis):
            self.buf, self.me, self.on_axis = buf, me, on_axis
            self.mid = buf.shape[1] // 2

        def start(self):
            mine = self.buf.at[self.me]
            self.right = send(mine, mine, self.on_axis(1))
            self.left = send(mine, mine, self.on_axis(-1))

        def forward(self):
            self.right.wait_recv()
            low = self.buf.at[at(self.me, -1), pl.ds(0, self.mid)]
            self.right2 = send(low, low, self.on_axis(1))
            self.left.wait_recv()
            high = self.buf.at[at(self.me, 1), pl.ds(self.mid, self.mid)]
            self.left2 = send(high, high, self.on_axis(-1))

        def finish(self):
            self.right2.wait_recv()
            self.left2.wait_recv()

    def transpose_slices(src, dst, dp_of):
        @pl.loop(0, ranks)
        def _(k):
            owner = dp_of(k)
            first = owner * sz.owned
            tile = jnp.minimum(first // 128, sz.last_tile)
            shift = first - tile * 128
            shape = (sz.owned_pad, sz.window)
            rows = lax.broadcasted_iota(jnp.int32, shape, 0)
            cols = lax.broadcasted_iota(jnp.int32, shape, 1)
            pick = jnp.where(cols == rows + shift, 1.0, 0.0).astype(BF16)
            part = src[:, pl.ds(pl.multiple_of(tile * 128, 128), sz.window)]
            dst[k] = lax.dot_general(
                pick, part, ROW_DIMS, preferred_element_type=F32
            ).astype(BF16)

    class SliceExchange:
        def __init__(self, src, dst, me, on_axis, sem):
            self.src, self.dst, self.me, self.on_axis = src, dst, me, on_axis
            self.sem = sem

        def start(self):
            pair = RING // 2
            self.direct = []
            for k in (1, -1, 2):
                piece = self.src.at[pl.ds(at(self.me, k) * RING + pair * c, pair)]
                place = self.dst.at[self.me, pl.ds(pair * c, pair)]
                self.direct.append(send(piece, place, self.on_axis(k)))
            self.local = pltpu.make_async_copy(
                self.src.at[pl.ds(self.me * RING, RING)], self.dst.at[self.me], self.sem
            )
            self.local.start()

        def share(self):
            pair = RING // 2
            self.shared = []
            for k, made in zip((1, -1, 2), self.direct):
                made.wait_recv()
                place = self.dst.at[at(self.me, -k), pl.ds(pair * c, pair)]
                self.shared.append(send(place, place, sibling))

        def finish(self):
            for made in self.shared:
                made.wait_recv()
            self.local.wait()

    class RingReduce:
        def __init__(self, part, out, into, me, on_axis, mid):
            self.part, self.out, self.into = part, out, into
            self.me, self.on_axis, self.mid = me, on_axis, mid
            self.count = part.shape[1]

        def start(self):
            lo, hi = pl.ds(0, self.mid), pl.ds(self.mid, self.count - self.mid)
            far, right, left = at(self.me, 2), at(self.me, 1), at(self.me, -1)
            out, into = self.out, self.into
            out[0, lo] = self.part[far, lo].astype(BF16)
            self.far_right = send(out.at[0, lo], into.at[0, lo], self.on_axis(1))
            out[0, hi] = self.part[far, hi].astype(BF16)
            self.far_left = send(out.at[0, hi], into.at[0, hi], self.on_axis(-1))
            out[1, hi] = self.part[right, hi].astype(BF16)
            self.near_right = send(out.at[1, hi], into.at[1, hi], self.on_axis(1))
            out[2, lo] = self.part[left, lo].astype(BF16)
            self.near_left = send(out.at[2, lo], into.at[2, lo], self.on_axis(-1))

        def forward(self):
            lo, hi = pl.ds(0, self.mid), pl.ds(self.mid, self.count - self.mid)
            right, left = at(self.me, 1), at(self.me, -1)
            out, into = self.out, self.into
            self.far_right.wait_recv()
            out[1, lo] = (self.part[right, lo] + into[0, lo].astype(F32)).astype(BF16)
            self.sum_right = send(out.at[1, lo], into.at[1, lo], self.on_axis(1))
            self.far_left.wait_recv()
            out[2, hi] = (self.part[left, hi] + into[0, hi].astype(F32)).astype(BF16)
            self.sum_left = send(out.at[2, hi], into.at[2, hi], self.on_axis(-1))

        def finish(self):
            self.near_right.wait_recv()
            self.near_left.wait_recv()
            self.sum_right.wait_recv()
            self.sum_left.wait_recv()

        def total(self):
            return (
                self.part[self.me]
                + self.into[1].astype(F32)
                + self.into[2].astype(F32)
            )

    class RowReduce:
        def __init__(self, index):
            self.index = index

        def multiply(self, lhs, weight):
            index = self.index

            @pl.loop(0, width // sz.chunk)
            def _(n):
                cols = pl.ds(pl.multiple_of(n * sz.chunk, sz.chunk), sz.chunk)
                full = lax.dot_general(
                    lhs[...], weight[cols, :], ROW_DIMS, preferred_element_type=F32
                )
                for k in range(RING):
                    even = full[2 * k * own : (2 * k + 1) * own]
                    odd = full[(2 * k + 1) * own : (2 * k + 2) * own]
                    row_sum[index, k, :, cols] = jnp.where(c == 0, even, odd)
                    sib_out[index, k, :, cols] = jnp.where(c == 0, odd, even).astype(BF16)

            self.copy = send(sib_out.at[index], sib_in.at[index], sibling)

        def start(self):
            index = self.index
            self.copy.wait_recv()
            row_sum[index] = row_sum[index] + sib_in[index].astype(F32)
            self.ring = RingReduce(
                row_sum.at[index], rs_out.at[index], rs_in.at[index], x, on_x, half
            )
            self.ring.start()

    def multiply_grad(index, lhs, rhs):
        @pl.loop(0, RING)
        def _(k):
            total = jnp.dot(lhs[0, k], rhs[0], preferred_element_type=F32)
            for g in range(1, RING):
                total += jnp.dot(lhs[g, k], rhs[g], preferred_element_type=F32)
            wg_sum[index, k] = total

    grad_rows = RowGather(grad_all)
    norm_rows = RowGather(norm_all)
    load_grad.wait()
    grad_rows.start()

    def pick(s, j):
        home = (dp - j + ranks) % ranks
        named = slot_ref[home * sz.homes + j]
        return jnp.where(named == dp * sz.slots + s, 1.0, 0.0).astype(F32)

    grad_rows.forward()
    for made in routed:
        made.wait_recv()
    for s in range(sz.slots):
        total = pick(s, 0) * tokens_ref[0].astype(F32)
        for j in range(1, sz.homes):
            total += pick(s, j) * arrived[j - 1].astype(F32)
        row_in[s * sz.block_rows : (s + 1) * sz.block_rows, :] = total
    rows_f = row_in[...]
    inv = lax.rsqrt(jnp.mean(rows_f * rows_f, axis=-1, keepdims=True) + 1e-06)
    inv_ref[...] = jnp.broadcast_to(inv, inv_ref.shape)
    norm_all[my_rows, :] = (rows_f * inv * gain_ref[...]).astype(BF16)
    norm_rows.start()

    grad_rows.finish()
    load_fc2.wait()

    def multiply_in(lhs, weight, out):
        @pl.loop(0, width // sz.chunk)
        def _(n):
            cols = pl.ds(pl.multiple_of(n * sz.chunk, sz.chunk), sz.chunk)
            part = jnp.dot(lhs[:, cols], weight[cols, :], preferred_element_type=F32)

            @pl.when(n == 0)
            def _():
                out[...] = part

            @pl.when(n > 0)
            def _():
                out[...] += part

    multiply_in(grad_all, fc2_ref, hid_grad)
    norm_rows.forward()
    transpose_slices(grad_all, grad_t, lambda k: k)
    grad_slices = SliceExchange(grad_t, grad_tg, y, on_y, local_sems.at[3])
    grad_slices.start()
    norm_rows.finish()

    load_fc1.wait()
    multiply_in(norm_all, fc1_ref, pre_act)

    @pl.loop(0, sz.rows // 16)
    def _(n):
        rows = pl.ds(pl.multiple_of(n * 16, 16), 16)
        value = pre_act[rows, :]
        cdf = 0.5 * (1.0 + lax.erf(value * 0.7071067811865476))
        slope = cdf + value * jnp.exp(-0.5 * value * value) * 0.3989422804014327
        hid_g[y, rows, :] = (value * cdf).astype(BF16)
        pre_g[z, rows, :] = (hid_grad[rows, :] * slope).astype(BF16)

    hid_ring = RingGather(hid_g, y, on_y)
    pre_ring = RingGather(pre_g, z, on_z)
    hid_ring.start()
    pre_ring.start()
    transpose_slices(norm_all, norm_t, lambda k: (k % RING) * RING + k // RING)
    norm_slices = SliceExchange(norm_t, norm_tg, z, on_z, local_sems.at[4])
    norm_slices.start()
    grad_slices.share()

    branch = RowReduce(0)
    branch.multiply(hid_g.at[y], fc2_ref)
    back = RowReduce(1)
    back.multiply(pre_g.at[z], fc1_ref)
    branch.start()
    hid_ring.forward()
    pre_ring.forward()
    back.start()
    norm_slices.share()
    branch.ring.forward()
    back.ring.forward()

    branch.ring.finish()
    mixed_ref[...] = (row_in[...] + branch.ring.total()).astype(BF16)

    back.ring.finish()
    normed_grad = back.ring.total()
    unit = row_in[...] * inv_ref[:, :1]
    product = normed_grad * unit
    gain_sib[0] = jnp.sum(product, axis=0, keepdims=True)
    gain_pair = send(gain_sib.at[0], gain_sib.at[1], sibling)
    scaled = normed_grad * gain_ref[...]
    inner = scaled - unit * jnp.mean(scaled * unit, axis=-1, keepdims=True)
    input_grad[...] = (
        grad_all[my_rows, :].astype(F32) + inv_ref[:, :1] * inner
    ).astype(BF16).astype(F32)

    returned = []
    for j in range(sz.homes):
        total = pick(0, j) * input_grad[0 : sz.block_rows, :]
        for s in range(1, sz.slots):
            total += pick(s, j) * input_grad[s * sz.block_rows : (s + 1) * sz.block_rows, :]
        if j == 0:
            tgrad_ref[0] = total.astype(BF16)
        else:
            back_out[j - 1] = total.astype(BF16)
            returned.append(send(back_out.at[j - 1], tgrad_ref.at[j], on_dp(-j)))

    hid_ring.finish()
    grad_slices.finish()
    multiply_grad(0, grad_tg, hid_g)
    mid = round_up(sz.owned_pad // 2, 16)
    fc2_ring = RingReduce(wg_sum.at[0], wg_out.at[0], wg_in.at[0], z, on_z, mid)
    fc2_ring.start()
    pre_ring.finish()
    norm_slices.finish()
    multiply_grad(1, norm_tg, pre_g)
    fc1_ring = RingReduce(wg_sum.at[1], wg_out.at[1], wg_in.at[1], y, on_y, mid)
    fc1_ring.start()

    gain_pair.wait_recv()
    total = gain_sib[0] + gain_sib[1]

    def add_over(buf, me, on_axis, total):
        buf[me] = total
        made = [send(buf.at[me], buf.at[me], on_axis(k)) for k in (1, -1, 2)]
        for one in made:
            one.wait_recv()
        return buf[0] + buf[1] + buf[2] + buf[3]

    total = add_over(gain_x, x, on_x, total)
    fc2_ring.forward()
    total = add_over(gain_y, y, on_y, total)
    fc1_ring.forward()
    total = add_over(gain_z, z, on_z, total)
    gain_grad_ref[...] = total

    fc2_ring.finish()
    fc2_grad_ref[...] = fc2_ring.total()[: sz.owned]
    fc1_ring.finish()
    fc1_grad_ref[...] = fc1_ring.total()[: sz.owned]
    for made in returned:
        made.wait_recv()
    for made in started:
        made.wait_send()
    if len(started) != copies:
        raise ValueError(len(started))


COPIES = 82


def local(tokens, norm_gain, fc1, fc2t, block_slot, out_grad):
    sz = Sizes(tokens.shape, fc1.shape, out_grad.shape)
    width, units = sz.width, sz.units
    vmem = pl.BlockSpec(memory_space=pltpu.VMEM)
    anywhere = pl.BlockSpec(memory_space=pl.ANY)
    slices = (RING, RING, sz.owned_pad, sz.rows)
    mixed, tgrad, fc1_grad, fc2_grad, gain_grad = pl.pallas_call(
        functools.partial(kernel, sz, COPIES),
        out_shape=(
            jax.ShapeDtypeStruct((sz.own, width), BF16),
            jax.ShapeDtypeStruct(tokens.shape, BF16),
            jax.ShapeDtypeStruct((sz.owned, units), F32),
            jax.ShapeDtypeStruct((sz.owned, units), F32),
            jax.ShapeDtypeStruct((1, width), F32),
        ),
        in_specs=[
            pl.BlockSpec(memory_space=pltpu.SMEM),
            vmem,
            vmem,
            anywhere,
            anywhere,
            anywhere,
        ],
        out_specs=(vmem,) * 5,
        scratch_shapes=[
            pltpu.VMEM(fc1.shape, BF16),
            pltpu.VMEM(fc2t.shape, BF16),
            pltpu.VMEM((sz.homes - 1, sz.block_rows, width), BF16),
            pltpu.VMEM((sz.own, width), F32),
            pltpu.VMEM((sz.own, 128), F32),
            pltpu.VMEM((sz.rows, width), BF16),
            pltpu.VMEM((sz.rows, width), BF16),
            pltpu.VMEM((RING * RING, sz.owned_pad, sz.rows), BF16),
            pltpu.VMEM((RING * RING, sz.owned_pad, sz.rows), BF16),
            pltpu.VMEM(slices, BF16),
            pltpu.VMEM(slices, BF16),
            pltpu.VMEM((RING, sz.rows, units), BF16),
            pltpu.VMEM((RING, sz.rows, units), BF16),
            pltpu.VMEM((sz.rows, units), F32),
            pltpu.VMEM((sz.rows, units), F32),
            pltpu.VMEM((2, RING, sz.own, width), F32),
            pltpu.VMEM((2, RING, sz.own, width), BF16),
            pltpu.VMEM((2, RING, sz.own, width), BF16),
            pltpu.VMEM((2, 3, sz.own, width), BF16),
            pltpu.VMEM((2, 3, sz.own, width), BF16),
            pltpu.VMEM((2, RING, sz.owned_pad, units), F32),
            pltpu.VMEM((2, 3, sz.owned_pad, units), BF16),
            pltpu.VMEM((2, 3, sz.owned_pad, units), BF16),
            pltpu.VMEM((sz.homes - 1, sz.block_rows, width), BF16),
            pltpu.VMEM((sz.own, width), F32),
            pltpu.VMEM((2, 1, width), F32),
            pltpu.VMEM((RING, 1, width), F32),
            pltpu.VMEM((RING, 1, width), F32),
            pltpu.VMEM((RING, 1, width), F32),
            pltpu.SemaphoreType.DMA((5,)),
            pltpu.SemaphoreType.DMA((COPIES,)),
            pltpu.SemaphoreType.DMA((COPIES,)),
        ],
        compiler_params=pltpu.CompilerParams(
            collective_id=0, has_side_effects=True, vmem_limit_bytes=60 * 1024 * 1024
        ),
        cost_estimate=pl.CostEstimate(
            flops=12 * sz.rows * width * units,
            bytes_accessed=4 * width * units,
            transcendentals=2 * sz.rows * units,
        ),
        name="mlp_block",
    )(
        block_slot,
        norm_gain.reshape(1, width),
        tokens,
        fc1,
        fc2t,
        out_grad.reshape(sz.own, width),
    )
    return (
        mixed.reshape(out_grad.shape),
        tgrad,
        fc1_grad,
        fc2_grad,
        gain_grad.reshape(width),
    )


def solution(mesh):
    placed = (
        P("dp", "tensor", None),
        P(),
        P(None, "tensor"),
        P(None, "tensor"),
        P(),
        P("dp", "tensor", None),
    )
    return jax.shard_map(
        local,
        mesh=mesh,
        in_specs=placed,
        out_specs=(
            P("dp", "tensor", None),
            P("dp", "tensor", None),
            P("dp", "tensor"),
            P("dp", "tensor"),
            P(),
        ),
        check_vma=False,
    )
```

time: 508 us -> 121 us (0.24)
  waiting for transfers between devices: 281 us -> 0 us
  Pallas kernels: 0 us -> 91.8 us
  blocking collectives: 66.5 us -> 0 us
  matrix products: 58.8 us -> 0 us
  local copies, waits for them, and re-layouts: 47.4 us -> 26.1 us
  starting transfers between devices: 18.2 us -> 0 us
  between operations: 14.9 us -> 0.64 us
  other arithmetic: 14.9 us -> 1.35 us
    unnamed x6 -> x0, waiting for transfers between devices: 210 us -> none
    pallas_call x0 -> x1, Pallas kernels: none -> 91.8 us  [local(): pl.pallas_call(functools.partial(kernel, sz, COPIES), out_shape=(jax.Shap...]
    psum x1 -> x0, blocking collectives: 66.5 us -> none  [local(): lax.psum(jnp.sum(normed_grad * unit_rows, axis=0), ('dp', 'tensor'))]
    dot_general x8 -> x0, matrix products: 58.8 us -> none  [the longest x1 14.7 us: local(): lax.dot_general(part_rows, fc2t, ROW_DIMS, preferred_element_type=jnp.flo...]
    another operation x8 -> x0, local copies, waits for them, and re-layouts: 39.5 us -> none  [the longest x1 36.3 us: local(): jnp.stack([first, second], axis=1)]
    all_gather x2 -> x0, waiting for transfers between devices: 38.3 us -> none  [the longest x1 24.6 us: local(): grad_all = lax.all_gather(grad_flat, 'tensor', axis=0, tiled=True)]
    reduce_scatter x2 -> x0, waiting for transfers between devices: 27.2 us -> none  [the longest x1 27.2 us: local(): lax.psum_scatter(lax.dot_general(part_rows, fc2t, ROW_DIMS, preferred_ele...]
    unnamed x31 -> x6, local copies, waits for them, and re-layouts: 3.24 us -> 24.8 us
  transfers between devices with their start and end apart: 13 -> 0, of which waited for: 8 -> 0; matrix products, arithmetic and copies ran while one was open for 19% -> 0% of each run, Pallas kernels for 0% -> 0%
where the time goes in v1:
time: 121 us; the launch traced here: 120 us
  Pallas kernels  91.8 us (76%)
  local copies, waits for them, and re-layouts  26.1 us (22%)
  other arithmetic  1.35 us (1%)
    pallas_call x1, Pallas kernels, local(): pl.pallas_call(functools.partial(kernel, sz, COPIES), out_shape=(jax.Shap...  91.8 us
    unnamed x6, local copies, waits for them, and re-layouts  24.8 us

profile of v1, /device:TPU:0, one launch (start us, length us, event | category | flops | bytes accessed | tf_op | source)
XLA Modules:
  0.0 119.9 jit_solution(7897163113448152102)
XLA Ops:
  0.6 1.3 %reshape.22.gain_ref = f32[1,3200]{1,0:T(1,128)} reshape(f32[3200]{0:T(1024)} %param.7) | data formatting | bytes 25600 | tf_op jit(solution)/shard_map/reshape | solution.py:560
  2.0 8.6 %copy.11.fc1_hbm = bf16[3200,800]{1,0:T(8,128)(2,1)} copy(bf16[3200,800]{0,1:T(8,128)(2,1)} %param.8) | data formatting | bytes 10240000 | tf_op args[2]
  10.6 8.6 %copy.12.fc2_hbm = bf16[3200,800]{1,0:T(8,128)(2,1)} copy(bf16[3200,800]{0,1:T(8,128)(2,1)} %param.9) | data formatting | bytes 10240000 | tf_op args[3]
  19.2 91.8 %mlp_block.1 = (bf16[32,3200]{1,0:T(8,128)(2,1)}, bf16[5,16,3200]{2,1,0:T(8,128)(2,1)}, f32[200,800]{1,0:T(8,128)}, f32[200,800]{1,0:T(8,128)}, f32[1,3200]{1,0:T(1,128)}) custom-call(s32[80]{0:T(128)} %slot_ref.1, f32[1,3200]{1,0:T(1,128)} %reshape.22.gain_ref, bf16[5,16,3200]{2,1,0:T(8,128)(2,1)} %tokens_ref.1, bf16[3200,800]{1,0:T(8,128)(2,1)} %copy.11.fc1_hbm, ...), custom_call_target="tpu_custom_call" | custom-call | flops 7864320000 | bytes 10240000 | tf_op jit(solution)/shard_map/mlp_block/pallas_call | solution.py:497
  111.1 1.4 %reduce = f32[3200]{0:T(1024)} reduce(f32[1,3200]{1,0:T(1,128)} %get-tuple-element.14, f32[]{:T(128)} %constant.2), dimensions={0}, to_apply=%get-tuple-element.14.reduce_sub_computation | reduce | bytes 25604 | tf_op jit(solution)/shard_map/mlp_block/pallas_call | solution.py:497
  112.4 1.6 %copy.17 = bf16[2,16,3200]{2,1,0:T(8,128)(2,1)} copy(bf16[2,16,3200]{2,1,0:T(8,128)(2,1)} %bitcast.2) | data formatting | bytes 409600
  114.0 1.9 %copy.18 = bf16[5,16,3200]{2,1,0:T(8,128)(2,1)} copy(bf16[5,16,3200]{2,1,0:T(8,128)(2,1)} %get-tuple-element.21) | data formatting | bytes 1024000
  115.9 2.0 %copy.19 = f32[200,800]{1,0:T(8,128)} copy(f32[200,800]{1,0:T(8,128)} %get-tuple-element.22) | data formatting | bytes 1280000
  117.9 2.0 %copy.20 = f32[200,800]{1,0:T(8,128)} copy(f32[200,800]{1,0:T(8,128)} %get-tuple-element.23) | data formatting | bytes 1280000

commit v2 on v1

--- a/solution.py
+++ b/solution.py
@@ -309,9 +309,7 @@
             @pl.loop(0, width // sz.chunk)
             def _(n):
                 cols = pl.ds(pl.multiple_of(n * sz.chunk, sz.chunk), sz.chunk)
-                full = lax.dot_general(
-                    lhs[...], weight[cols, :], ROW_DIMS, preferred_element_type=F32
-                )
+                full = jnp.dot(lhs[...], weight[:, cols], preferred_element_type=F32)
                 for k in range(RING):
                     even = full[2 * k * own : (2 * k + 1) * own]
                     odd = full[(2 * k + 1) * own : (2 * k + 2) * own]
@@ -358,7 +356,7 @@
     rows_f = row_in[...]
     inv = lax.rsqrt(jnp.mean(rows_f * rows_f, axis=-1, keepdims=True) + 1e-06)
     inv_ref[...] = jnp.broadcast_to(inv, inv_ref.shape)
-    norm_all[my_rows, :] = (rows_f * inv * gain_ref[...]).astype(BF16)
+    norm_all[my_rows, :] = (rows_f * inv * gain_ref[...].reshape(1, width)).astype(BF16)
     norm_rows.start()
 
     grad_rows.finish()
@@ -368,7 +366,9 @@
         @pl.loop(0, width // sz.chunk)
         def _(n):
             cols = pl.ds(pl.multiple_of(n * sz.chunk, sz.chunk), sz.chunk)
-            part = jnp.dot(lhs[:, cols], weight[cols, :], preferred_element_type=F32)
+            part = lax.dot_general(
+                lhs[:, cols], weight[:, cols], ROW_DIMS, preferred_element_type=F32
+            )
 
             @pl.when(n == 0)
             def _():
@@ -427,7 +427,7 @@
     product = normed_grad * unit
     gain_sib[0] = jnp.sum(product, axis=0, keepdims=True)
     gain_pair = send(gain_sib.at[0], gain_sib.at[1], sibling)
-    scaled = normed_grad * gain_ref[...]
+    scaled = normed_grad * gain_ref[...].reshape(1, width)
     inner = scaled - unit * jnp.mean(scaled * unit, axis=-1, keepdims=True)
     input_grad[...] = (
         grad_all[my_rows, :].astype(F32) + inv_ref[:, :1] * inner
@@ -471,7 +471,7 @@
     total = add_over(gain_y, y, on_y, total)
     fc1_ring.forward()
     total = add_over(gain_z, z, on_z, total)
-    gain_grad_ref[...] = total
+    gain_grad_ref[...] = total.reshape(width)
 
     fc2_ring.finish()
     fc2_grad_ref[...] = fc2_ring.total()[: sz.owned]
@@ -483,6 +483,31 @@
         made.wait_send()
     if len(started) != copies:
         raise ValueError(len(started))
+
+
+def hand_over_kernel(*refs):
+    count = len(refs) // 2
+    sems = refs[-1]
+    made = [
+        pltpu.make_async_copy(refs[i], refs[count + i], sems.at[i]) for i in range(count)
+    ]
+    for one in made:
+        one.start()
+    for one in made:
+        one.wait()
+
+
+def hand_over(*arrays):
+    anywhere = pl.BlockSpec(memory_space=pl.ANY)
+    return pl.pallas_call(
+        hand_over_kernel,
+        out_shape=tuple(jax.ShapeDtypeStruct(a.shape, a.dtype) for a in arrays),
+        in_specs=[anywhere] * len(arrays),
+        out_specs=(anywhere,) * len(arrays),
+        scratch_shapes=[pltpu.SemaphoreType.DMA((len(arrays),))],
+        compiler_params=pltpu.CompilerParams(vmem_limit_bytes=60 * 1024 * 1024),
+        name="hand_over",
+    )(*arrays)
 
 
 COPIES = 82
@@ -501,7 +526,7 @@
             jax.ShapeDtypeStruct(tokens.shape, BF16),
             jax.ShapeDtypeStruct((sz.owned, units), F32),
             jax.ShapeDtypeStruct((sz.owned, units), F32),
-            jax.ShapeDtypeStruct((1, width), F32),
+            jax.ShapeDtypeStruct((width,), F32),
         ),
         in_specs=[
             pl.BlockSpec(memory_space=pltpu.SMEM),
@@ -513,8 +538,8 @@
         ],
         out_specs=(vmem,) * 5,
         scratch_shapes=[
-            pltpu.VMEM(fc1.shape, BF16),
-            pltpu.VMEM(fc2t.shape, BF16),
+            pltpu.VMEM((units, width), BF16),
+            pltpu.VMEM((units, width), BF16),
             pltpu.VMEM((sz.homes - 1, sz.block_rows, width), BF16),
             pltpu.VMEM((sz.own, width), F32),
             pltpu.VMEM((sz.own, 128), F32),
@@ -557,19 +582,16 @@
         name="mlp_block",
     )(
         block_slot,
-        norm_gain.reshape(1, width),
+        norm_gain,
         tokens,
-        fc1,
-        fc2t,
+        fc1.T,
+        fc2t.T,
         out_grad.reshape(sz.own, width),
     )
-    return (
-        mixed.reshape(out_grad.shape),
-        tgrad,
-        fc1_grad,
-        fc2_grad,
-        gain_grad.reshape(width),
+    mixed, tgrad, fc1_grad, fc2_grad, gain_grad = hand_over(
+        mixed, tgrad, fc1_grad, fc2_grad, gain_grad
     )
+    return mixed.reshape(out_grad.shape), tgrad, fc1_grad, fc2_grad, gain_grad
 
 
 def solution(mesh):

time: 121 us -> 159 us (1.31)
  Pallas kernels: 91.8 us -> 158 us
  local copies, waits for them, and re-layouts: 26.1 us -> 0 us
    pallas_call x0 -> x1, Pallas kernels: none -> 66.7 us  [hand_over(): pl.pallas_call(hand_over_kernel, out_shape=tuple((jax.ShapeDtypeStruct(a....]
    unnamed x6 -> x0, local copies, waits for them, and re-layouts: 24.8 us -> none
where the time goes in v2:
time: 159 us; the launch traced here: 158 us
  Pallas kernels  158 us (99%)
    pallas_call x1, Pallas kernels, local(): pl.pallas_call(functools.partial(kernel, sz, COPIES), out_shape=(jax.Shap...  91.2 us
    pallas_call x1, Pallas kernels, hand_over(): pl.pallas_call(hand_over_kernel, out_shape=tuple((jax.ShapeDtypeStruct(a....  66.7 us

profile of v2, /device:TPU:0, one launch (start us, length us, event | category | flops | bytes accessed | tf_op | source)
XLA Modules:
  0.0 158.5 jit_solution(7559353215867320167)
XLA Ops:
  0.6 91.2 %mlp_block.1 = (bf16[32,3200]{1,0:T(8,128)(2,1)}, bf16[5,16,3200]{2,1,0:T(8,128)(2,1)}, f32[200,800]{1,0:T(8,128)}, f32[200,800]{1,0:T(8,128)}, f32[3200]{0:T(1024)}) custom-call(s32[80]{0:T(128)} %slot_ref.1, f32[3200]{0:T(1024)} %gain_ref.1, bf16[5,16,3200]{2,1,0:T(8,128)(2,1)} %tokens_ref.1, bf16[800,3200]{1,0:T(8,128)(2,1)} %bitcast.4, ...), custom_call_target="tpu_custom_call" | custom-call | flops 7864320000 | bytes 10240000 | tf_op jit(solution)/shard_map/mlp_block/pallas_call | solution.py:522
  91.8 66.7 %hand_over.1 = (bf16[32,3200]{1,0:T(8,128)(2,1)}, bf16[5,16,3200]{2,1,0:T(8,128)(2,1)}, f32[200,800]{1,0:T(8,128)}, f32[200,800]{1,0:T(8,128)}, f32[3200]{0:T(1024)}) custom-call(bf16[32,3200]{1,0:T(8,128)(2,1)} %get-tuple-element.15.refs_0_, bf16[5,16,3200]{2,1,0:T(8,128)(2,1)} %get-tuple-element.16.refs_1_, f32[200,800]{1,0:T(8,128)} %get-tuple-element.17.refs_2_, ...), custom_call_target="tpu_custom_call" | custom-call | tf_op jit(solution)/shard_map/hand_over/pallas_call | solution.py:502

commit v3 on v2

v3 whole, which is shorter than its diff:
```python
import functools

import jax
import jax.numpy as jnp
from jax import lax
from jax.experimental import pallas as pl
from jax.experimental.pallas import tpu as pltpu
from jax.sharding import PartitionSpec as P

MESH = pl.DeviceIdType.MESH
ROW_DIMS = (((1,), (1,)), ((), ()))
RING = 4
RANKS = RING * RING
F32 = jnp.float32
BF16 = jnp.bfloat16

STEP = (0, -1, 1, 2)


def round_up(value, unit):
    return (value + unit - 1) // unit * unit


def chunk_of(width, limit):
    tiles = width // 128
    best = 1
    for count in range(1, tiles + 1):
        if tiles % count == 0 and count * 128 <= limit:
            best = count
    return best * 128


class Sizes:
    def __init__(self, tokens, fc1, out_grad):
        self.homes, self.block_rows, self.width = tokens
        self.units = fc1[1]
        self.slots = out_grad[0]
        self.own = self.slots * self.block_rows
        self.pair = 2 * self.own
        self.rows = RING * self.pair
        self.owned = self.width // RANKS
        self.owned_pad = round_up(self.owned, 16)
        self.group = RING * self.owned
        self.group_step = self.group // 128 * 128
        self.group_pad = round_up(self.group + (RING - 1) * (self.group - self.group_step), 128)
        self.sum_rows = self.group_pad + 8
        self.chunk = chunk_of(self.width, 640)
        first = round_up(self.units // 2, 128) - 128
        self.parts = ((0, first), (first, self.units - first))
        self.part_max = max(count for _, count in self.parts)


def kernel(
    sz,
    copies,
    slot_ref,
    gain_ref,
    tokens_hbm,
    fc1_hbm,
    fc2_hbm,
    grad_hbm,
    mixed_ref,
    tgrad_ref,
    fc1_grad_ref,
    fc2_grad_ref,
    gain_grad_ref,
    fc1_ref,
    fc2_ref,
    arrived,
    row_in,
    inv_ref,
    grad_all,
    norm_all,
    norm_cut,
    grad_sl,
    norm_sl,
    grad_t,
    norm_t,
    hid_g,
    pre_g,
    hid_n,
    pre_n,
    pre_act,
    hid_grad,
    row_sum,
    sib_out,
    sib_in,
    rs_out,
    rs_in,
    wg_sum,
    wg_out,
    wg_in,
    back_out,
    input_grad,
    gain_sib,
    gain_x,
    gain_y,
    gain_z,
    local_sems,
    send_sems,
    recv_sems,
):
    dp = lax.axis_index("dp")
    t = lax.axis_index("tensor")
    y, z = dp // RING, dp % RING
    x, c = t // 2, t % 2
    own, width = sz.own, sz.width
    half = own // 2
    gain = gain_ref[...].reshape(1, width)

    def on_dp(k):
        return ((dp + k + RANKS) % RANKS, t)

    def on_x(k):
        return (dp, ((x + k + RING) % RING) * 2 + c)

    def on_y(k):
        return (((y + k + RING) % RING) * RING + z, t)

    def on_z(k):
        return (y * RING + (z + k + RING) % RING, t)

    sibling = (dp, t + 1 - 2 * c)

    started = []

    def send(src, dst, device):
        index = len(started)
        made = pltpu.make_async_remote_copy(
            src_ref=src,
            dst_ref=dst,
            send_sem=send_sems.at[index],
            recv_sem=recv_sems.at[index],
            device_id=device,
            device_id_type=MESH,
        )
        made.start()
        started.append(made)
        return made

    my_rows = pl.ds(pl.multiple_of(c * own, own), own)
    load_grad = pltpu.make_async_copy(grad_hbm, grad_all.at[my_rows], local_sems.at[0])
    load_token = pltpu.make_async_copy(tokens_hbm.at[0], arrived.at[0], local_sems.at[1])
    load_fc2 = pltpu.make_async_copy(fc2_hbm, fc2_ref, local_sems.at[2])
    load_fc1 = pltpu.make_async_copy(fc1_hbm, fc1_ref, local_sems.at[3])
    load_grad.start()
    load_token.start()
    load_fc2.start()
    load_fc1.start()

    partners = [on_dp(k) for k in range(1, sz.homes)]
    partners += [on_dp(-k) for k in range(1, sz.homes)]
    partners += [on_y(k) for k in (1, -1, 2)]
    partners += [on_z(k) for k in (1, -1, 2)]
    partners += [on_x(k) for k in (1, -1, 2)]
    partners += [sibling]
    barrier = pltpu.get_barrier_semaphore()
    for device in partners:
        pl.semaphore_signal(barrier, inc=1, device_id=device, device_id_type=MESH)
    pl.semaphore_wait(barrier, len(partners))

    class RowGather:
        def __init__(self, view):
            self.view = view

        def part(self, slot, lo, count):
            place = sz.pair * slot + c * own + lo
            return self.view(pl.ds(pl.multiple_of(place, 16), count))

        def start(self):
            mine = self.part(0, 0, own)
            self.right = send(mine, self.part(1, 0, own), on_x(1))
            self.left = send(mine, self.part(2, 0, own), on_x(-1))
            self.shared = [send(mine, mine, sibling)]

        def forward(self):
            self.right.wait_recv()
            self.right2 = send(self.part(1, 0, half), self.part(3, 0, half), on_x(1))
            whole = self.part(1, 0, own)
            self.shared.append(send(whole, whole, sibling))
            self.left.wait_recv()
            rest = own - half
            self.left2 = send(self.part(2, half, rest), self.part(3, half, rest), on_x(-1))
            whole = self.part(2, 0, own)
            self.shared.append(send(whole, whole, sibling))

        def finish(self):
            self.right2.wait_recv()
            low = self.part(3, 0, half)
            self.shared.append(send(low, low, sibling))
            self.left2.wait_recv()
            high = self.part(3, half, own - half)
            self.shared.append(send(high, high, sibling))
            for made in self.shared:
                made.wait_recv()

    class RingGather:
        def __init__(self, buf, lo, count, on_axis):
            self.buf, self.on_axis = buf, on_axis
            self.whole = pl.ds(lo, count)
            self.low = pl.ds(lo, count // 2)
            self.high = pl.ds(lo + count // 2, count // 2)

        def start(self):
            buf, on_axis = self.buf, self.on_axis
            mine = buf.at[0, self.whole]
            self.right = send(mine, buf.at[1, self.whole], on_axis(1))
            self.left = send(mine, buf.at[2, self.whole], on_axis(-1))

        def forward(self):
            buf, on_axis = self.buf, self.on_axis
            self.right.wait_recv()
            self.right2 = send(buf.at[1, self.low], buf.at[3, self.low], on_axis(1))
            self.left.wait_recv()
            self.left2 = send(buf.at[2, self.high], buf.at[3, self.high], on_axis(-1))

        def finish(self):
            self.right2.wait_recv()
            self.left2.wait_recv()

    class RingReduce:
        def __init__(self, part, out, into, on_axis, mid, count):
            self.part, self.out, self.into = part, out, into
            self.on_axis, self.mid, self.count = on_axis, mid, count

        def start(self):
            mid, rest = self.mid, self.count - self.mid
            lo, hi = pl.ds(0, mid), pl.ds(mid, rest)
            part, out, into, on_axis = self.part, self.out, self.into, self.on_axis
            out[0, lo] = part(3, 0, mid).astype(BF16)
            self.far_right = send(out.at[0, lo], into.at[0, lo], on_axis(1))
            out[0, hi] = part(3, mid, rest).astype(BF16)
            self.far_left = send(out.at[0, hi], into.at[0, hi], on_axis(-1))
            out[1, hi] = part(2, mid, rest).astype(BF16)
            self.near_right = send(out.at[1, hi], into.at[1, hi], on_axis(1))
            out[2, lo] = part(1, 0, mid).astype(BF16)
            self.near_left = send(out.at[2, lo], into.at[2, lo], on_axis(-1))

        def forward(self):
            mid, rest = self.mid, self.count - self.mid
            lo, hi = pl.ds(0, mid), pl.ds(mid, rest)
            part, out, into, on_axis = self.part, self.out, self.into, self.on_axis
            self.far_right.wait_recv()
            out[1, lo] = (part(2, 0, mid) + into[0, lo].astype(F32)).astype(BF16)
            self.sum_right = send(out.at[1, lo], into.at[1, lo], on_axis(1))
            self.far_left.wait_recv()
            out[2, hi] = (part(1, mid, rest) + into[0, hi].astype(F32)).astype(BF16)
            self.sum_left = send(out.at[2, hi], into.at[2, hi], on_axis(-1))

        def finish(self):
            self.near_right.wait_recv()
            self.near_left.wait_recv()
            self.sum_right.wait_recv()
            self.sum_left.wait_recv()

        def total(self):
            first = self.part(0, 0, self.count) + self.into[1].astype(F32)
            return first + self.into[2].astype(F32)

    class RowReduce:
        def __init__(self, index):
            self.index = index

        def multiply(self, lhs, weight, also=None):
            index = self.index

            @pl.loop(0, width // sz.chunk)
            def _(n):
                cols = pl.ds(pl.multiple_of(n * sz.chunk, sz.chunk), sz.chunk)
                full = jnp.dot(lhs[...], weight[:, cols], preferred_element_type=F32)
                for k in range(RING):
                    even = full[sz.pair * k : sz.pair * k + own]
                    odd = full[sz.pair * k + own : sz.pair * (k + 1)]
                    row_sum[index, k, :, cols] = jnp.where(c == 0, even, odd)
                    sib_out[index, k, :, cols] = jnp.where(c == 0, odd, even).astype(BF16)
                if also is not None:
                    also(cols, full)

            self.copy = send(sib_out.at[index], sib_in.at[index], sibling)

        def start(self):
            index = self.index
            self.copy.wait_recv()
            row_sum[index] = row_sum[index] + sib_in[index].astype(F32)

            def part(k, lo, count):
                return row_sum[index, k, lo : lo + count]

            self.ring = RingReduce(part, rs_out.at[index], rs_in.at[index], on_x, half, own)
            self.ring.start()

    class WeightGrad:
        def __init__(self, index, p, slices, blocks, on_axis, owner_row, out):
            self.index, self.p, self.out = index, p, out
            self.slices, self.blocks = slices, blocks
            self.lo, self.units = sz.parts[p]
            self.on_axis, self.owner_row = on_axis, owner_row

        def multiply(self):
            index, p, lo, units = self.index, self.p, self.lo, self.units
            step = sz.group_pad // RING

            @pl.loop(0, RING)
            def _(m):
                rows = pl.ds(pl.multiple_of(m * step, step), step)
                total = None
                for k in range(RING):
                    one = lax.dot_general(
                        self.slices[k, rows, :],
                        self.blocks[k, lo : lo + units, :],
                        ROW_DIMS,
                        preferred_element_type=F32,
                    )
                    total = one if total is None else total + one
                wg_sum[index, p, rows, 0:units] = total

            wg_sum[index, p, sz.group_pad : sz.sum_rows, 0:units] = jnp.zeros((8, units), F32)

            def part(k, first, count):
                place = pl.multiple_of(self.owner_row(k) + first, 8)
                return wg_sum[index, p, pl.ds(place, count), 0:units]

            self.ring = RingReduce(
                part,
                wg_out.at[index, p, :, :, pl.ds(0, units)],
                wg_in.at[index, p, :, :, pl.ds(0, units)],
                self.on_axis,
                round_up(sz.owned_pad // 2, 16),
                sz.owned_pad,
            )
            self.ring.start()

        def finish(self):
            self.ring.finish()
            self.out[:, self.lo : self.lo + self.units] = self.ring.total()[: sz.owned]

    grad_rows = RowGather(lambda rows: grad_all.at[rows])
    norm_rows = RowGather(lambda rows: norm_all.at[rows])
    cut_rows = RowGather(lambda rows: norm_sl.at[pl.ds(1, RING - 1), rows])
    routed = [send(tokens_hbm.at[j], arrived.at[j], on_dp(j)) for j in range(1, sz.homes)]
    load_grad.wait()
    grad_rows.start()

    def pick(s, j):
        home = (dp - j + RANKS) % RANKS
        named = slot_ref[home * sz.homes + j]
        return jnp.where(named == dp * sz.slots + s, 1.0, 0.0).astype(F32)

    def group_columns(rows, q):
        cuts = []
        for k in range(RING):
            first = sz.owned * (RING * k + q)
            cuts.append(rows[:, first : first + sz.owned])
        cuts.append(jnp.zeros((rows.shape[0], sz.group_pad - sz.group), rows.dtype))
        return jnp.concatenate(cuts, axis=1)

    load_token.wait()
    for made in routed:
        made.wait_recv()
    for s in range(sz.slots):
        total = pick(s, 0) * arrived[0].astype(F32)
        for j in range(1, sz.homes):
            total += pick(s, j) * arrived[j].astype(F32)
        row_in[s * sz.block_rows : (s + 1) * sz.block_rows, :] = total
    rows_f = row_in[...]
    inv = lax.rsqrt(jnp.mean(rows_f * rows_f, axis=-1, keepdims=True) + 1e-06)
    inv_ref[...] = jnp.broadcast_to(inv, inv_ref.shape)
    norm_own = (rows_f * inv * gain).astype(BF16)
    norm_all[my_rows, :] = norm_own
    norm_rows.start()
    grad_rows.forward()
    for q in range(RING):
        norm_cut[q] = group_columns(norm_own, q)
    cut_sent = []
    for k, slot in ((1, 1), (-1, 2), (2, 3)):
        cut_sent.append(
            send(norm_cut.at[(z + k + RING) % RING], norm_sl.at[slot, my_rows], on_z(k))
        )

    grad_rows.finish()
    side = sz.rows // 2
    side_rows = pl.ds(pl.multiple_of(c * side, side), side)
    slice_sent = []
    for k, slot in ((1, 1), (-1, 2), (2, 3)):
        first = pl.multiple_of(((y + k + RING) % RING) * sz.group_step, 128)
        slice_sent.append(
            send(
                grad_all.at[side_rows, pl.ds(first, sz.group_pad)],
                grad_sl.at[slot, side_rows],
                on_y(k),
            )
        )

    load_fc2.wait()

    def multiply_in(lhs, lo, count, rows, out):
        @pl.loop(0, width // sz.chunk)
        def _(n):
            cols = pl.ds(pl.multiple_of(n * sz.chunk, sz.chunk), sz.chunk)
            part = lax.dot_general(
                lhs[lo : lo + count, cols], rows[:, cols], ROW_DIMS, preferred_element_type=F32
            )

            @pl.when(n == 0)
            def _():
                out[lo : lo + count, :] = part

            @pl.when(n > 0)
            def _():
                out[lo : lo + count, :] += part

    multiply_in(fc2_ref, *sz.parts[0], grad_all, hid_grad)
    norm_rows.forward()
    multiply_in(fc2_ref, *sz.parts[1], grad_all, hid_grad)
    own_first = pl.multiple_of(y * sz.group_step, 128)
    grad_t[0] = grad_all[:, pl.ds(own_first, sz.group_pad)].T
    load_fc1.wait()
    norm_rows.finish()
    for made in cut_sent:
        made.wait_recv()
    cut_rows.start()

    hid_ring, pre_ring = [], []
    for lo, count in sz.parts:
        multiply_in(fc1_ref, lo, count, norm_all, pre_act)

        @pl.loop(0, count // 32)
        def _(n):
            rows = pl.ds(pl.multiple_of(lo + n * 32, 32), 32)
            value = pre_act[rows, :]
            cdf = 0.5 * (1.0 + lax.erf(value * 0.7071067811865476))
            slope = cdf + value * jnp.exp(-0.5 * value * value) * 0.3989422804014327
            hid_g[0, rows, :] = (value * cdf).astype(BF16)
            pre_g[0, rows, :] = (hid_grad[rows, :] * slope).astype(BF16)

        hid_ring.append(RingGather(hid_g, lo, count, on_y))
        pre_ring.append(RingGather(pre_g, lo, count, on_z))
        hid_ring[-1].start()
        pre_ring[-1].start()

    slice_shared = []
    for slot, made in zip((1, 2, 3), slice_sent):
        made.wait_recv()
        place = grad_sl.at[slot, side_rows]
        slice_shared.append(send(place, place, sibling))
    cut_rows.forward()
    hid_ring[0].forward()
    pre_ring[0].forward()

    back = RowReduce(1)
    branch = RowReduce(0)
    pre_n[...] = pre_g[0].T

    def gain_part(cols, full):
        product = full * norm_all[:, cols].astype(F32)
        gain_sib[0, :, cols] = jnp.sum(product, axis=0, keepdims=True)

    back.multiply(pre_n, fc1_ref, gain_part)
    gain_pair = send(gain_sib.at[0], gain_sib.at[1], sibling)
    cut_rows.finish()
    hid_ring[1].forward()
    pre_ring[1].forward()
    back.start()
    hid_n[...] = hid_g[0].T
    branch.multiply(hid_n, fc2_ref)
    for made in slice_shared:
        made.wait_recv()
    for k in range(1, RING):
        grad_t[k] = grad_sl[k].T

    def add_start(buf, me, on_axis, total):
        buf[me] = total
        return [send(buf.at[me], buf.at[me], on_axis(k)) for k in (1, -1, 2)]

    def add_finish(buf, made):
        for one in made:
            one.wait_recv()
        return buf[0] + buf[1] + buf[2] + buf[3]

    gain_pair.wait_recv()
    adding = add_start(gain_x, x, on_x, gain_sib[0] + gain_sib[1])
    back.ring.forward()
    branch.start()

    def fc2_row(k):
        return y * (sz.group - sz.group_step) + ((z + STEP[k] + RING) % RING) * sz.owned

    def fc1_row(k):
        return ((y + STEP[k] + RING) % RING) * sz.owned

    fc2_grad = [
        WeightGrad(0, p, grad_t, hid_g, on_z, fc2_row, fc2_grad_ref) for p in range(2)
    ]
    fc1_grad = [
        WeightGrad(1, p, norm_t, pre_g, on_y, fc1_row, fc1_grad_ref) for p in range(2)
    ]
    hid_ring[0].finish()
    fc2_grad[0].multiply()

    for q in range(RING):

        @pl.when(z == q)
        def _():
            norm_t[0] = group_columns(norm_all[...], q).T

    for k in range(1, RING):
        norm_t[k] = norm_sl[k].T
    pre_ring[0].finish()
    fc1_grad[0].multiply()
    branch.ring.forward()
    back.ring.finish()

    normed_grad = back.ring.total()
    unit = row_in[...] * inv_ref[:, :1]
    scaled = normed_grad * gain
    inner = scaled - unit * jnp.mean(scaled * unit, axis=-1, keepdims=True)
    input_grad[...] = (
        (grad_all[my_rows, :].astype(F32) + inv_ref[:, :1] * inner).astype(BF16).astype(F32)
    )
    returned = []
    for j in range(sz.homes):
        total = pick(0, j) * input_grad[0 : sz.block_rows, :]
        for s in range(1, sz.slots):
            total += pick(s, j) * input_grad[s * sz.block_rows : (s + 1) * sz.block_rows, :]
        if j == 0:
            tgrad_ref[0] = total.astype(BF16)
        else:
            back_out[j - 1] = total.astype(BF16)
            returned.append(send(back_out.at[j - 1], tgrad_ref.at[j], on_dp(-j)))

    total = add_finish(gain_x, adding)
    adding = add_start(gain_y, y, on_y, total)
    fc2_grad[0].ring.forward()
    hid_ring[1].finish()
    fc2_grad[1].multiply()
    fc1_grad[0].ring.forward()
    pre_ring[1].finish()
    fc1_grad[1].multiply()
    total = add_finish(gain_y, adding)
    adding = add_start(gain_z, z, on_z, total)
    branch.ring.finish()
    mixed_ref[...] = (row_in[...] + branch.ring.total()).astype(BF16)
    fc2_grad[0].finish()
    fc2_grad[1].ring.forward()
    fc1_grad[0].finish()
    fc1_grad[1].ring.forward()
    total = add_finish(gain_z, adding)
    gain_grad_ref[...] = (total / gain).reshape(width)
    fc2_grad[1].finish()
    fc1_grad[1].finish()
    for made in returned:
        made.wait_recv()
    for made in started:
        made.wait_send()
    if len(started) != copies:
        raise ValueError(len(started))


def hand_over_kernel(*refs):
    count = len(refs) // 2
    sems = refs[-1]
    made = [
        pltpu.make_async_copy(refs[i], refs[count + i], sems.at[i]) for i in range(count)
    ]
    for one in made:
        one.start()
    for one in made:
        one.wait()


def hand_over(*arrays):
    anywhere = pl.BlockSpec(memory_space=pl.ANY)
    return pl.pallas_call(
        hand_over_kernel,
        out_shape=tuple(jax.ShapeDtypeStruct(a.shape, a.dtype) for a in arrays),
        in_specs=[anywhere] * len(arrays),
        out_specs=(pl.BlockSpec(memory_space=pltpu.VMEM),) * len(arrays),
        scratch_shapes=[pltpu.SemaphoreType.DMA((len(arrays),))],
        compiler_params=pltpu.CompilerParams(vmem_limit_bytes=60 * 1024 * 1024),
        name="hand_over",
    )(*arrays)


COPIES = 108


def local(tokens, norm_gain, fc1, fc2t, block_slot, out_grad):
    sz = Sizes(tokens.shape, fc1.shape, out_grad.shape)
    width, units = sz.width, sz.units
    vmem = pl.BlockSpec(memory_space=pltpu.VMEM)
    anywhere = pl.BlockSpec(memory_space=pl.ANY)
    slices = (RING, sz.rows, sz.group_pad)
    slices_t = (RING, sz.group_pad, sz.rows)
    pieces = (2, 2, 3, sz.owned_pad, sz.part_max)
    arrays = pl.pallas_call(
        functools.partial(kernel, sz, COPIES),
        out_shape=(
            jax.ShapeDtypeStruct((sz.own, width), BF16),
            jax.ShapeDtypeStruct(tokens.shape, BF16),
            jax.ShapeDtypeStruct((sz.owned, units), F32),
            jax.ShapeDtypeStruct((sz.owned, units), F32),
            jax.ShapeDtypeStruct((width,), F32),
        ),
        in_specs=[
            pl.BlockSpec(memory_space=pltpu.SMEM),
            vmem,
            anywhere,
            anywhere,
            anywhere,
            anywhere,
        ],
        out_specs=(vmem,) * 5,
        scratch_shapes=[
            pltpu.VMEM((units, width), BF16),
            pltpu.VMEM((units, width), BF16),
            pltpu.VMEM(tokens.shape, BF16),
            pltpu.VMEM((sz.own, width), F32),
            pltpu.VMEM((sz.own, 128), F32),
            pltpu.VMEM((sz.rows, width), BF16),
            pltpu.VMEM((sz.rows, width), BF16),
            pltpu.VMEM((RING, sz.own, sz.group_pad), BF16),
            pltpu.VMEM(slices, BF16),
            pltpu.VMEM(slices, BF16),
            pltpu.VMEM(slices_t, BF16),
            pltpu.VMEM(slices_t, BF16),
            pltpu.VMEM((RING, units, sz.rows), BF16),
            pltpu.VMEM((RING, units, sz.rows), BF16),
            pltpu.VMEM((sz.rows, units), BF16),
            pltpu.VMEM((sz.rows, units), BF16),
            pltpu.VMEM((units, sz.rows), F32),
            pltpu.VMEM((units, sz.rows), F32),
            pltpu.VMEM((2, RING, sz.own, width), F32),
            pltpu.VMEM((2, RING, sz.own, width), BF16),
            pltpu.VMEM((2, RING, sz.own, width), BF16),
            pltpu.VMEM((2, 3, sz.own, width), BF16),
            pltpu.VMEM((2, 3, sz.own, width), BF16),
            pltpu.VMEM((2, 2, sz.sum_rows, sz.part_max), F32),
            pltpu.VMEM(pieces, BF16),
            pltpu.VMEM(pieces, BF16),
            pltpu.VMEM((sz.homes - 1, sz.block_rows, width), BF16),
            pltpu.VMEM((sz.own, width), F32),
            pltpu.VMEM((2, 1, width), F32),
            pltpu.VMEM((RING, 1, width), F32),
            pltpu.VMEM((RING, 1, width), F32),
            pltpu.VMEM((RING, 1, width), F32),
            pltpu.SemaphoreType.DMA((4,)),
            pltpu.SemaphoreType.DMA((COPIES,)),
            pltpu.SemaphoreType.DMA((COPIES,)),
        ],
        compiler_params=pltpu.CompilerParams(
            collective_id=0, has_side_effects=True, vmem_limit_bytes=60 * 1024 * 1024
        ),
        cost_estimate=pl.CostEstimate(
            flops=12 * sz.rows * width * units,
            bytes_accessed=4 * width * units,
            transcendentals=2 * sz.rows * units,
        ),
        name="mlp_block",
    )(
        block_slot,
        norm_gain,
        tokens,
        fc1.T,
        fc2t.T,
        out_grad.reshape(sz.own, width),
    )
    mixed, tgrad, fc1_grad, fc2_grad, gain_grad = hand_over(*arrays)
    return mixed.reshape(out_grad.shape), tgrad, fc1_grad, fc2_grad, gain_grad


def solution(mesh):
    placed = (
        P("dp", "tensor", None),
        P(),
        P(None, "tensor"),
        P(None, "tensor"),
        P(),
        P("dp", "tensor", None),
    )
    return jax.shard_map(
        local,
        mesh=mesh,
        in_specs=placed,
        out_specs=(
            P("dp", "tensor", None),
            P("dp", "tensor", None),
            P("dp", "tensor"),
            P("dp", "tensor"),
            P(),
        ),
        check_vma=False,
    )
```

time: 159 us -> 90.3 us (0.57)
  Pallas kernels: 158 us -> 89 us
    pallas_call x1, Pallas kernels: 66.7 us -> 2.97 us  [hand_over(): pl.pallas_call(hand_over_kernel, out_shape=tuple((jax.ShapeDtypeStruct(a....]
    pallas_call x1, Pallas kernels: 91.2 us -> 86.1 us  [local(): pl.pallas_call(functools.partial(kernel, sz, COPIES), out_shape=(jax.Shap...]
where the time goes in v3:
time: 90.3 us; the launch traced here: 89.7 us
  Pallas kernels  89 us (99%)
    pallas_call x1, Pallas kernels, local(): pl.pallas_call(functools.partial(kernel, sz, COPIES), out_shape=(jax.Shap...  86.1 us
    pallas_call x1, Pallas kernels, hand_over(): pl.pallas_call(hand_over_kernel, out_shape=tuple((jax.ShapeDtypeStruct(a....  2.97 us

profile of v3, /device:TPU:0, one launch (start us, length us, event | category | flops | bytes accessed | tf_op | source)
XLA Modules:
  0.0 89.7 jit_solution(14163404232999464638)
XLA Ops:
  0.6 86.1 %mlp_block.1 = (bf16[32,3200]{1,0:T(8,128)(2,1)}, bf16[5,16,3200]{2,1,0:T(8,128)(2,1)}, f32[200,800]{1,0:T(8,128)}, f32[200,800]{1,0:T(8,128)}, f32[3200]{0:T(1024)}) custom-call(s32[80]{0:T(128)} %slot_ref.1, f32[3200]{0:T(1024)} %gain_ref.1, bf16[5,16,3200]{2,1,0:T(8,128)(2,1)} %tokens_hbm.1, bf16[800,3200]{1,0:T(8,128)(2,1)} %bitcast.4, ...), custom_call_target="tpu_custom_call" | custom-call | flops 7864320000 | bytes 10240000 | tf_op jit(solution)/shard_map/mlp_block/pallas_call | solution.py:595
  86.7 3.0 %hand_over.1 = (bf16[32,3200]{1,0:T(8,128)(2,1)}, bf16[5,16,3200]{2,1,0:T(8,128)(2,1)}, f32[200,800]{1,0:T(8,128)}, f32[200,800]{1,0:T(8,128)}, f32[3200]{0:T(1024)}) custom-call(bf16[32,3200]{1,0:T(8,128)(2,1)} %get-tuple-element.15.refs_0_, bf16[5,16,3200]{2,1,0:T(8,128)(2,1)} %get-tuple-element.16.refs_1_, f32[200,800]{1,0:T(8,128)} %get-tuple-element.17.refs_2_, ...), custom_call_target="tpu_custom_call" | custom-call | tf_op jit(solution)/shard_map/hand_over/pallas_call | solution.py:573

commit v4 on v3

--- a/solution.py
+++ b/solution.py
@@ -47,6 +47,8 @@
         self.chunk = chunk_of(self.width, 640)
         first = round_up(self.units // 2, 128) - 128
         self.parts = ((0, first), (first, self.units - first))
+        mid = round_up(self.width // 2, 128)
+        self.cuts = ((0, mid), (mid, self.width - mid))
         self.part_max = max(count for _, count in self.parts)
 
 
@@ -67,7 +69,7 @@
     fc1_ref,
     fc2_ref,
     arrived,
-    row_in,
+    row_all,
     inv_ref,
     grad_all,
     norm_all,
@@ -335,9 +337,12 @@
             self.out[:, self.lo : self.lo + self.units] = self.ring.total()[: sz.owned]
 
     grad_rows = RowGather(lambda rows: grad_all.at[rows])
-    norm_rows = RowGather(lambda rows: norm_all.at[rows])
     cut_rows = RowGather(lambda rows: norm_sl.at[pl.ds(1, RING - 1), rows])
-    routed = [send(tokens_hbm.at[j], arrived.at[j], on_dp(j)) for j in range(1, sz.homes)]
+    routed = []
+    for lo, count in sz.cuts:
+        cols = pl.ds(lo, count)
+        for j in range(1, sz.homes):
+            routed.append(send(tokens_hbm.at[j, :, cols], arrived.at[j, :, cols], on_dp(j)))
     load_grad.wait()
     grad_rows.start()
 
@@ -355,20 +360,32 @@
         return jnp.concatenate(cuts, axis=1)
 
     load_token.wait()
-    for made in routed:
-        made.wait_recv()
-    for s in range(sz.slots):
-        total = pick(s, 0) * arrived[0].astype(F32)
-        for j in range(1, sz.homes):
-            total += pick(s, j) * arrived[j].astype(F32)
-        row_in[s * sz.block_rows : (s + 1) * sz.block_rows, :] = total
-    rows_f = row_in[...]
-    inv = lax.rsqrt(jnp.mean(rows_f * rows_f, axis=-1, keepdims=True) + 1e-06)
+    row_parts = []
+    for n, (lo, count) in enumerate(sz.cuts):
+        cols = slice(lo, lo + count)
+        for made in routed[n * (sz.homes - 1) : (n + 1) * (sz.homes - 1)]:
+            made.wait_recv()
+        for s in range(sz.slots):
+            total = pick(s, 0) * arrived[0, :, cols].astype(F32)
+            for j in range(1, sz.homes):
+                total += pick(s, j) * arrived[j, :, cols].astype(F32)
+            place = c * own + s * sz.block_rows
+            rows = pl.ds(pl.multiple_of(place, sz.block_rows), sz.block_rows)
+            row_all[rows, cols] = total.astype(BF16)
+        one = RowGather(lambda rows, lo=lo, count=count: row_all.at[rows, pl.ds(lo, count)])
+        one.start()
+        row_parts.append(one)
+        if n == 0:
+            grad_rows.forward()
+
+    def normed_rows(rows):
+        value = row_all[rows, :].astype(F32)
+        inv = lax.rsqrt(jnp.mean(value * value, axis=-1, keepdims=True) + 1e-06)
+        return value * inv, inv
+
+    unit_own, inv = normed_rows(my_rows)
     inv_ref[...] = jnp.broadcast_to(inv, inv_ref.shape)
-    norm_own = (rows_f * inv * gain).astype(BF16)
-    norm_all[my_rows, :] = norm_own
-    norm_rows.start()
-    grad_rows.forward()
+    norm_own = (unit_own * gain).astype(BF16)
     for q in range(RING):
         norm_cut[q] = group_columns(norm_own, q)
     cut_sent = []
@@ -377,6 +394,7 @@
             send(norm_cut.at[(z + k + RING) % RING], norm_sl.at[slot, my_rows], on_z(k))
         )
 
+    row_parts[0].forward()
     grad_rows.finish()
     side = sz.rows // 2
     side_rows = pl.ds(pl.multiple_of(c * side, side), side)
@@ -409,16 +427,23 @@
             def _():
                 out[lo : lo + count, :] += part
 
+    row_parts[1].forward()
     multiply_in(fc2_ref, *sz.parts[0], grad_all, hid_grad)
-    norm_rows.forward()
     multiply_in(fc2_ref, *sz.parts[1], grad_all, hid_grad)
     own_first = pl.multiple_of(y * sz.group_step, 128)
     grad_t[0] = grad_all[:, pl.ds(own_first, sz.group_pad)].T
     load_fc1.wait()
-    norm_rows.finish()
+    row_parts[0].finish()
+    row_parts[1].finish()
     for made in cut_sent:
         made.wait_recv()
     cut_rows.start()
+
+    @pl.loop(0, sz.rows // 16)
+    def _(n):
+        rows = pl.ds(pl.multiple_of(n * 16, 16), 16)
+        unit, _ = normed_rows(rows)
+        norm_all[rows, :] = (unit * gain).astype(BF16)
 
     hid_ring, pre_ring = [], []
     for lo, count in sz.parts:
@@ -511,7 +536,7 @@
     back.ring.finish()
 
     normed_grad = back.ring.total()
-    unit = row_in[...] * inv_ref[:, :1]
+    unit = row_all[my_rows, :].astype(F32) * inv_ref[:, :1]
     scaled = normed_grad * gain
     inner = scaled - unit * jnp.mean(scaled * unit, axis=-1, keepdims=True)
     input_grad[...] = (
@@ -539,7 +564,7 @@
     total = add_finish(gain_y, adding)
     adding = add_start(gain_z, z, on_z, total)
     branch.ring.finish()
-    mixed_ref[...] = (row_in[...] + branch.ring.total()).astype(BF16)
+    mixed_ref[...] = (row_all[my_rows, :].astype(F32) + branch.ring.total()).astype(BF16)
     fc2_grad[0].finish()
     fc2_grad[1].ring.forward()
     fc1_grad[0].finish()
@@ -557,14 +582,19 @@
 
 
 def hand_over_kernel(*refs):
-    count = len(refs) // 2
-    sems = refs[-1]
-    made = [
-        pltpu.make_async_copy(refs[i], refs[count + i], sems.at[i]) for i in range(count)
-    ]
-    for one in made:
+    count = (len(refs) - 2) // 3
+    source, target, held = refs[:count], refs[count : 2 * count], refs[2 * count : 3 * count]
+    in_sems, out_sems = refs[-2:]
+    loads, stores = [], []
+    for i in range(count):
+        loads.append(pltpu.make_async_copy(source[i], held[i], in_sems.at[i]))
+        stores.append(pltpu.make_async_copy(held[i], target[i], out_sems.at[i]))
+    for one in loads:
         one.start()
-    for one in made:
+    for load, store in zip(loads, stores):
+        load.wait()
+        store.start()
+    for one in stores:
         one.wait()
 
 
@@ -574,14 +604,15 @@
         hand_over_kernel,
         out_shape=tuple(jax.ShapeDtypeStruct(a.shape, a.dtype) for a in arrays),
         in_specs=[anywhere] * len(arrays),
-        out_specs=(pl.BlockSpec(memory_space=pltpu.VMEM),) * len(arrays),
-        scratch_shapes=[pltpu.SemaphoreType.DMA((len(arrays),))],
+        out_specs=(anywhere,) * len(arrays),
+        scratch_shapes=[pltpu.VMEM(a.shape, a.dtype) for a in arrays]
+        + [pltpu.SemaphoreType.DMA((len(arrays),))] * 2,
         compiler_params=pltpu.CompilerParams(vmem_limit_bytes=60 * 1024 * 1024),
         name="hand_over",
     )(*arrays)
 
 
-COPIES = 108
+COPIES = 121
 
 
 def local(tokens, norm_gain, fc1, fc2t, block_slot, out_grad):
@@ -614,7 +645,7 @@
             pltpu.VMEM((units, width), BF16),
             pltpu.VMEM((units, width), BF16),
             pltpu.VMEM(tokens.shape, BF16),
-            pltpu.VMEM((sz.own, width), F32),
+            pltpu.VMEM((sz.rows, width), BF16),
             pltpu.VMEM((sz.own, 128), F32),
             pltpu.VMEM((sz.rows, width), BF16),
             pltpu.VMEM((sz.rows, width), BF16),

time: 90.3 us -> 87.1 us (0.965)
  Pallas kernels: 89 us -> 85.8 us
    pallas_call x1, Pallas kernels: 86.1 us -> 83.3 us  [local(): pl.pallas_call(functools.partial(kernel, sz, COPIES), out_shape=(jax.Shap...]
where the time goes in v4:
time: 87.1 us; the launch traced here: 86.5 us
  Pallas kernels  85.8 us (99%)
    pallas_call x1, Pallas kernels, local(): pl.pallas_call(functools.partial(kernel, sz, COPIES), out_shape=(jax.Shap...  83.3 us
    pallas_call x1, Pallas kernels, hand_over(): pl.pallas_call(hand_over_kernel, out_shape=tuple((jax.ShapeDtypeStruct(a....  2.56 us

profile of v4, /device:TPU:0, one launch (start us, length us, event | category | flops | bytes accessed | tf_op | source)
XLA Modules:
  0.0 86.5 jit_solution(11420825291512450502)
XLA Ops:
  0.6 83.3 %mlp_block.1 = (bf16[32,3200]{1,0:T(8,128)(2,1)}, bf16[5,16,3200]{2,1,0:T(8,128)(2,1)}, f32[200,800]{1,0:T(8,128)}, f32[200,800]{1,0:T(8,128)}, f32[3200]{0:T(1024)}) custom-call(s32[80]{0:T(128)} %slot_ref.1, f32[3200]{0:T(1024)} %gain_ref.1, bf16[5,16,3200]{2,1,0:T(8,128)(2,1)} %tokens_hbm.1, bf16[800,3200]{1,0:T(8,128)(2,1)} %bitcast.4, ...), custom_call_target="tpu_custom_call" | custom-call | flops 7864320000 | bytes 10240000 | tf_op jit(solution)/shard_map/mlp_block/pallas_call | solution.py:626
  83.9 2.6 %hand_over.1 = (bf16[32,3200]{1,0:T(8,128)(2,1)}, bf16[5,16,3200]{2,1,0:T(8,128)(2,1)}, f32[200,800]{1,0:T(8,128)}, f32[200,800]{1,0:T(8,128)}, f32[3200]{0:T(1024)}) custom-call(bf16[32,3200]{1,0:T(8,128)(2,1)} %get-tuple-element.15.refs_0_, bf16[5,16,3200]{2,1,0:T(8,128)(2,1)} %get-tuple-element.16.refs_1_, f32[200,800]{1,0:T(8,128)} %get-tuple-element.17.refs_2_, ...), custom_call_target="tpu_custom_call" | custom-call | tf_op jit(solution)/shard_map/hand_over/pallas_call | solution.py:603

commit v5 on v4

--- a/solution.py
+++ b/solution.py
@@ -186,14 +186,16 @@
             whole = self.part(2, 0, own)
             self.shared.append(send(whole, whole, sibling))
 
-        def finish(self):
+        def last(self):
             self.right2.wait_recv()
             low = self.part(3, 0, half)
             self.shared.append(send(low, low, sibling))
             self.left2.wait_recv()
             high = self.part(3, half, own - half)
             self.shared.append(send(high, high, sibling))
-            for made in self.shared:
+
+        def wait(self, first, stop):
+            for made in self.shared[first:stop]:
                 made.wait_recv()
 
     class RingGather:
@@ -360,6 +362,7 @@
         return jnp.concatenate(cuts, axis=1)
 
     load_token.wait()
+    grad_rows.forward()
     row_parts = []
     for n, (lo, count) in enumerate(sz.cuts):
         cols = slice(lo, lo + count)
@@ -375,13 +378,20 @@
         one = RowGather(lambda rows, lo=lo, count=count: row_all.at[rows, pl.ds(lo, count)])
         one.start()
         row_parts.append(one)
-        if n == 0:
-            grad_rows.forward()
+    row_parts[0].forward()
+    grad_rows.last()
 
     def normed_rows(rows):
         value = row_all[rows, :].astype(F32)
         inv = lax.rsqrt(jnp.mean(value * value, axis=-1, keepdims=True) + 1e-06)
         return value * inv, inv
+
+    def norm_range(first, stop):
+        @pl.loop(first // 16, stop // 16)
+        def _(n):
+            rows = pl.ds(pl.multiple_of(n * 16, 16), 16)
+            unit, _ = normed_rows(rows)
+            norm_all[rows, :] = (unit * gain).astype(BF16)
 
     unit_own, inv = normed_rows(my_rows)
     inv_ref[...] = jnp.broadcast_to(inv, inv_ref.shape)
@@ -393,9 +403,8 @@
         cut_sent.append(
             send(norm_cut.at[(z + k + RING) % RING], norm_sl.at[slot, my_rows], on_z(k))
         )
-
-    row_parts[0].forward()
-    grad_rows.finish()
+    row_parts[1].forward()
+    grad_rows.wait(0, 5)
     side = sz.rows // 2
     side_rows = pl.ds(pl.multiple_of(c * side, side), side)
     slice_sent = []
@@ -408,6 +417,7 @@
                 on_y(k),
             )
         )
+    row_parts[0].last()
 
     load_fc2.wait()
 
@@ -427,23 +437,19 @@
             def _():
                 out[lo : lo + count, :] += part
 
-    row_parts[1].forward()
     multiply_in(fc2_ref, *sz.parts[0], grad_all, hid_grad)
+    row_parts[1].last()
     multiply_in(fc2_ref, *sz.parts[1], grad_all, hid_grad)
-    own_first = pl.multiple_of(y * sz.group_step, 128)
-    grad_t[0] = grad_all[:, pl.ds(own_first, sz.group_pad)].T
-    load_fc1.wait()
-    row_parts[0].finish()
-    row_parts[1].finish()
+    for one in row_parts:
+        one.wait(0, 3)
+    norm_range(0, 3 * sz.pair)
     for made in cut_sent:
         made.wait_recv()
+    for one in row_parts:
+        one.wait(3, 5)
     cut_rows.start()
-
-    @pl.loop(0, sz.rows // 16)
-    def _(n):
-        rows = pl.ds(pl.multiple_of(n * 16, 16), 16)
-        unit, _ = normed_rows(rows)
-        norm_all[rows, :] = (unit * gain).astype(BF16)
+    norm_range(3 * sz.pair, sz.rows)
+    load_fc1.wait()
 
     hid_ring, pre_ring = [], []
     for lo, count in sz.parts:
@@ -482,12 +488,15 @@
 
     back.multiply(pre_n, fc1_ref, gain_part)
     gain_pair = send(gain_sib.at[0], gain_sib.at[1], sibling)
-    cut_rows.finish()
+    cut_rows.last()
     hid_ring[1].forward()
     pre_ring[1].forward()
     back.start()
     hid_n[...] = hid_g[0].T
     branch.multiply(hid_n, fc2_ref)
+    cut_rows.wait(0, 5)
+    own_first = pl.multiple_of(y * sz.group_step, 128)
+    grad_t[0] = grad_all[:, pl.ds(own_first, sz.group_pad)].T
     for made in slice_shared:
         made.wait_recv()
     for k in range(1, RING):

time: 87.1 us -> 87.9 us (level)
  no operation moved by 1% of the time
where the time goes in v5:
time: 87.9 us; the launch traced here: 86.9 us
  Pallas kernels  86.3 us (98%)
    pallas_call x1, Pallas kernels, local(): pl.pallas_call(functools.partial(kernel, sz, COPIES), out_shape=(jax.Shap...  83.7 us
    pallas_call x1, Pallas kernels, hand_over(): pl.pallas_call(hand_over_kernel, out_shape=tuple((jax.ShapeDtypeStruct(a....  2.56 us

profile of v5, /device:TPU:0, one launch (start us, length us, event | category | flops | bytes accessed | tf_op | source)
XLA Modules:
  0.0 86.9 jit_solution(4585308660724101161)
XLA Ops:
  0.6 83.7 %mlp_block.1 = (bf16[32,3200]{1,0:T(8,128)(2,1)}, bf16[5,16,3200]{2,1,0:T(8,128)(2,1)}, f32[200,800]{1,0:T(8,128)}, f32[200,800]{1,0:T(8,128)}, f32[3200]{0:T(1024)}) custom-call(s32[80]{0:T(128)} %slot_ref.1, f32[3200]{0:T(1024)} %gain_ref.1, bf16[5,16,3200]{2,1,0:T(8,128)(2,1)} %tokens_hbm.1, bf16[800,3200]{1,0:T(8,128)(2,1)} %bitcast.4, ...), custom_call_target="tpu_custom_call" | custom-call | flops 7864320000 | bytes 10240000 | tf_op jit(solution)/shard_map/mlp_block/pallas_call | solution.py:635
  84.4 2.6 %hand_over.1 = (bf16[32,3200]{1,0:T(8,128)(2,1)}, bf16[5,16,3200]{2,1,0:T(8,128)(2,1)}, f32[200,800]{1,0:T(8,128)}, f32[200,800]{1,0:T(8,128)}, f32[3200]{0:T(1024)}) custom-call(bf16[32,3200]{1,0:T(8,128)(2,1)} %get-tuple-element.15.refs_0_, bf16[5,16,3200]{2,1,0:T(8,128)(2,1)} %get-tuple-element.16.refs_1_, f32[200,800]{1,0:T(8,128)} %get-tuple-element.17.refs_2_, ...), custom_call_target="tpu_custom_call" | custom-call | tf_op jit(solution)/shard_map/hand_over/pallas_call | solution.py:612

commit v6 on v5

--- a/solution.py
+++ b/solution.py
@@ -302,9 +302,9 @@
 
         def multiply(self):
             index, p, lo, units = self.index, self.p, self.lo, self.units
-            step = sz.group_pad // RING
-
-            @pl.loop(0, RING)
+            step = sz.group_pad // 2
+
+            @pl.loop(0, 2)
             def _(m):
                 rows = pl.ds(pl.multiple_of(m * step, step), step)
                 total = None
@@ -469,32 +469,30 @@
         hid_ring[-1].start()
         pre_ring[-1].start()
 
+    back = RowReduce(1)
+    branch = RowReduce(0)
+
+    def gain_part(cols, full):
+        product = full * norm_all[:, cols].astype(F32)
+        gain_sib[0, :, cols] = jnp.sum(product, axis=0, keepdims=True)
+
+    pre_n[...] = pre_g[0].T
+    back.multiply(pre_n, fc1_ref, gain_part)
+    gain_pair = send(gain_sib.at[0], gain_sib.at[1], sibling)
+    hid_ring[0].forward()
+    pre_ring[0].forward()
+    cut_rows.forward()
     slice_shared = []
     for slot, made in zip((1, 2, 3), slice_sent):
         made.wait_recv()
         place = grad_sl.at[slot, side_rows]
         slice_shared.append(send(place, place, sibling))
-    cut_rows.forward()
-    hid_ring[0].forward()
-    pre_ring[0].forward()
-
-    back = RowReduce(1)
-    branch = RowReduce(0)
-    pre_n[...] = pre_g[0].T
-
-    def gain_part(cols, full):
-        product = full * norm_all[:, cols].astype(F32)
-        gain_sib[0, :, cols] = jnp.sum(product, axis=0, keepdims=True)
-
-    back.multiply(pre_n, fc1_ref, gain_part)
-    gain_pair = send(gain_sib.at[0], gain_sib.at[1], sibling)
-    cut_rows.last()
+    hid_n[...] = hid_g[0].T
+    branch.multiply(hid_n, fc2_ref)
+    back.start()
     hid_ring[1].forward()
     pre_ring[1].forward()
-    back.start()
-    hid_n[...] = hid_g[0].T
-    branch.multiply(hid_n, fc2_ref)
-    cut_rows.wait(0, 5)
+    cut_rows.last()
     own_first = pl.multiple_of(y * sz.group_step, 128)
     grad_t[0] = grad_all[:, pl.ds(own_first, sz.group_pad)].T
     for made in slice_shared:
@@ -511,10 +509,10 @@
             one.wait_recv()
         return buf[0] + buf[1] + buf[2] + buf[3]
 
+    branch.start()
+    back.ring.forward()
     gain_pair.wait_recv()
     adding = add_start(gain_x, x, on_x, gain_sib[0] + gain_sib[1])
-    back.ring.forward()
-    branch.start()
 
     def fc2_row(k):
         return y * (sz.group - sz.group_step) + ((z + STEP[k] + RING) % RING) * sz.owned
@@ -530,7 +528,7 @@
     ]
     hid_ring[0].finish()
     fc2_grad[0].multiply()
-
+    cut_rows.wait(0, 5)
     for q in range(RING):
 
         @pl.when(z == q)
@@ -542,6 +540,12 @@
     pre_ring[0].finish()
     fc1_grad[0].multiply()
     branch.ring.forward()
+    total = add_finish(gain_x, adding)
+    adding = add_start(gain_y, y, on_y, total)
+    fc2_grad[0].ring.forward()
+    hid_ring[1].finish()
+    fc2_grad[1].multiply()
+    fc1_grad[0].ring.forward()
     back.ring.finish()
 
     normed_grad = back.ring.total()
@@ -562,12 +566,6 @@
             back_out[j - 1] = total.astype(BF16)
             returned.append(send(back_out.at[j - 1], tgrad_ref.at[j], on_dp(-j)))
 
-    total = add_finish(gain_x, adding)
-    adding = add_start(gain_y, y, on_y, total)
-    fc2_grad[0].ring.forward()
-    hid_ring[1].finish()
-    fc2_grad[1].multiply()
-    fc1_grad[0].ring.forward()
     pre_ring[1].finish()
     fc1_grad[1].multiply()
     total = add_finish(gain_y, adding)

time: 87.9 us -> 85.9 us (0.977)
  Pallas kernels: 86.3 us -> 85.1 us
    pallas_call x1, Pallas kernels: 83.7 us -> 82.5 us  [local(): pl.pallas_call(functools.partial(kernel, sz, COPIES), out_shape=(jax.Shap...]
where the time goes in v6:
time: 85.9 us; the launch traced here: 85.7 us
  Pallas kernels  85.1 us (99%)
    pallas_call x1, Pallas kernels, local(): pl.pallas_call(functools.partial(kernel, sz, COPIES), out_shape=(jax.Shap...  82.5 us
    pallas_call x1, Pallas kernels, hand_over(): pl.pallas_call(hand_over_kernel, out_shape=tuple((jax.ShapeDtypeStruct(a....  2.56 us

profile of v6, /device:TPU:0, one launch (start us, length us, event | category | flops | bytes accessed | tf_op | source)
XLA Modules:
  0.0 85.7 jit_solution(3566632237976968561)
XLA Ops:
  0.6 82.5 %mlp_block.1 = (bf16[32,3200]{1,0:T(8,128)(2,1)}, bf16[5,16,3200]{2,1,0:T(8,128)(2,1)}, f32[200,800]{1,0:T(8,128)}, f32[200,800]{1,0:T(8,128)}, f32[3200]{0:T(1024)}) custom-call(s32[80]{0:T(128)} %slot_ref.1, f32[3200]{0:T(1024)} %gain_ref.1, bf16[5,16,3200]{2,1,0:T(8,128)(2,1)} %tokens_hbm.1, bf16[800,3200]{1,0:T(8,128)(2,1)} %bitcast.4, ...), custom_call_target="tpu_custom_call" | custom-call | flops 7864320000 | bytes 10240000 | tf_op jit(solution)/shard_map/mlp_block/pallas_call | solution.py:633
  83.2 2.6 %hand_over.1 = (bf16[32,3200]{1,0:T(8,128)(2,1)}, bf16[5,16,3200]{2,1,0:T(8,128)(2,1)}, f32[200,800]{1,0:T(8,128)}, f32[200,800]{1,0:T(8,128)}, f32[3200]{0:T(1024)}) custom-call(bf16[32,3200]{1,0:T(8,128)(2,1)} %get-tuple-element.15.refs_0_, bf16[5,16,3200]{2,1,0:T(8,128)(2,1)} %get-tuple-element.16.refs_1_, f32[200,800]{1,0:T(8,128)} %get-tuple-element.17.refs_2_, ...), custom_call_target="tpu_custom_call" | custom-call | tf_op jit(solution)/shard_map/hand_over/pallas_call | solution.py:610

commit v7 on v6

--- a/solution.py
+++ b/solution.py
@@ -69,6 +69,13 @@
     fc1_ref,
     fc2_ref,
     arrived,
+    midway,
+    midway_back,
+    mixed,
+    tgrad,
+    fc1_out,
+    fc2_out,
+    gain_out,
     row_all,
     inv_ref,
     grad_all,
@@ -99,6 +106,7 @@
     gain_y,
     gain_z,
     local_sems,
+    store_sems,
     send_sems,
     recv_sems,
 ):
@@ -126,7 +134,17 @@
 
     started = []
 
-    def send(src, dst, device):
+    class Guarded:
+        def __init__(self, made, when, arrives):
+            self.made, self.when, self.arrives = made, when, arrives
+
+        def wait_recv(self):
+            pl.when(self.arrives)(self.made.wait_recv)
+
+        def wait_send(self):
+            pl.when(self.when)(self.made.wait_send)
+
+    def send(src, dst, device, when=None, arrives=None):
         index = len(started)
         made = pltpu.make_async_remote_copy(
             src_ref=src,
@@ -136,7 +154,11 @@
             device_id=device,
             device_id_type=MESH,
         )
-        made.start()
+        if when is None:
+            made.start()
+        else:
+            pl.when(when)(made.start)
+            made = Guarded(made, when, when if arrives is None else arrives)
         started.append(made)
         return made
 
@@ -340,11 +362,17 @@
 
     grad_rows = RowGather(lambda rows: grad_all.at[rows])
     cut_rows = RowGather(lambda rows: norm_sl.at[pl.ds(1, RING - 1), rows])
-    routed = []
-    for lo, count in sz.cuts:
-        cols = pl.ds(lo, count)
-        for j in range(1, sz.homes):
-            routed.append(send(tokens_hbm.at[j, :, cols], arrived.at[j, :, cols], on_dp(j)))
+    (lo0, count0), (lo1, count1) = sz.cuts
+    cols0, cols1 = pl.ds(lo0, count0), pl.ds(lo1, count1)
+    via = []
+    for j in range(1, RING):
+        via.append(send(tokens_hbm.at[j, :, cols1], midway.at[j - 1], on_z(j)))
+    direct = []
+    for j in range(1, sz.homes):
+        direct.append(send(tokens_hbm.at[j, :, cols0], arrived.at[j, :, cols0], on_dp(j)))
+    last = []
+    for j in range(RING, sz.homes):
+        last.append(send(tokens_hbm.at[j, :, cols1], arrived.at[j, :, cols1], on_dp(j)))
     load_grad.wait()
     grad_rows.start()
 
@@ -361,12 +389,23 @@
         cuts.append(jnp.zeros((rows.shape[0], sz.group_pad - sz.group), rows.dtype))
         return jnp.concatenate(cuts, axis=1)
 
+    for j in range(1, RING):
+        via[j - 1].wait_recv()
+        last.append(
+            send(midway.at[j - 1], arrived.at[j, :, cols1], on_y(1), when=z < j)
+        )
+
+        @pl.when(z >= j)
+        def _():
+            arrived[j, :, lo1:] = midway[j - 1]
+
+    routed = (direct, last)
     load_token.wait()
     grad_rows.forward()
     row_parts = []
     for n, (lo, count) in enumerate(sz.cuts):
         cols = slice(lo, lo + count)
-        for made in routed[n * (sz.homes - 1) : (n + 1) * (sz.homes - 1)]:
+        for made in routed[n]:
             made.wait_recv()
         for s in range(sz.slots):
             total = pick(s, 0) * arrived[0, :, cols].astype(F32)
@@ -509,11 +548,6 @@
             one.wait_recv()
         return buf[0] + buf[1] + buf[2] + buf[3]
 
-    branch.start()
-    back.ring.forward()
-    gain_pair.wait_recv()
-    adding = add_start(gain_x, x, on_x, gain_sib[0] + gain_sib[1])
-
     def fc2_row(k):
         return y * (sz.group - sz.group_step) + ((z + STEP[k] + RING) % RING) * sz.owned
 
@@ -521,13 +555,17 @@
         return ((y + STEP[k] + RING) % RING) * sz.owned
 
     fc2_grad = [
-        WeightGrad(0, p, grad_t, hid_g, on_z, fc2_row, fc2_grad_ref) for p in range(2)
+        WeightGrad(0, p, grad_t, hid_g, on_z, fc2_row, fc2_out) for p in range(2)
     ]
     fc1_grad = [
-        WeightGrad(1, p, norm_t, pre_g, on_y, fc1_row, fc1_grad_ref) for p in range(2)
+        WeightGrad(1, p, norm_t, pre_g, on_y, fc1_row, fc1_out) for p in range(2)
     ]
     hid_ring[0].finish()
     fc2_grad[0].multiply()
+    back.ring.forward()
+    branch.start()
+    gain_pair.wait_recv()
+    adding = add_start(gain_x, x, on_x, gain_sib[0] + gain_sib[1])
     cut_rows.wait(0, 5)
     for q in range(RING):
 
@@ -539,13 +577,13 @@
         norm_t[k] = norm_sl[k].T
     pre_ring[0].finish()
     fc1_grad[0].multiply()
-    branch.ring.forward()
+    hid_ring[1].finish()
+    fc2_grad[1].multiply()
+    fc2_grad[0].ring.forward()
+    pre_ring[1].finish()
+    fc1_grad[1].multiply()
     total = add_finish(gain_x, adding)
     adding = add_start(gain_y, y, on_y, total)
-    fc2_grad[0].ring.forward()
-    hid_ring[1].finish()
-    fc2_grad[1].multiply()
-    fc1_grad[0].ring.forward()
     back.ring.finish()
 
     normed_grad = back.ring.total()
@@ -555,33 +593,64 @@
     input_grad[...] = (
         (grad_all[my_rows, :].astype(F32) + inv_ref[:, :1] * inner).astype(BF16).astype(F32)
     )
-    returned = []
+    returned, via = [], []
     for j in range(sz.homes):
         total = pick(0, j) * input_grad[0 : sz.block_rows, :]
         for s in range(1, sz.slots):
             total += pick(s, j) * input_grad[s * sz.block_rows : (s + 1) * sz.block_rows, :]
+        total = total.astype(BF16)
         if j == 0:
-            tgrad_ref[0] = total.astype(BF16)
+            tgrad[0] = total
+            continue
+        back_out[j - 1] = total
+        source, place = back_out.at[j - 1], tgrad.at[j]
+        if j < RING:
+            via.append(send(source.at[:, cols1], midway_back.at[j - 1], on_z(-j)))
+            returned.append(send(source.at[:, cols0], place.at[:, cols0], on_dp(-j)))
         else:
-            back_out[j - 1] = total.astype(BF16)
-            returned.append(send(back_out.at[j - 1], tgrad_ref.at[j], on_dp(-j)))
-
-    pre_ring[1].finish()
-    fc1_grad[1].multiply()
+            returned.append(send(source, place, on_dp(-j)))
+    branch.ring.forward()
+    fc1_grad[0].ring.forward()
     total = add_finish(gain_y, adding)
     adding = add_start(gain_z, z, on_z, total)
+    for j in range(1, RING):
+        via[j - 1].wait_recv()
+        returned.append(
+            send(midway_back.at[j - 1], tgrad.at[j, :, cols1], on_y(-1), when=z + j >= RING)
+        )
+
+        @pl.when(z + j < RING)
+        def _():
+            tgrad[j, :, lo1:] = midway_back[j - 1]
+
+    fc2_grad[1].ring.forward()
+    fc1_grad[1].ring.forward()
     branch.ring.finish()
-    mixed_ref[...] = (row_all[my_rows, :].astype(F32) + branch.ring.total()).astype(BF16)
-    fc2_grad[0].finish()
-    fc2_grad[1].ring.forward()
-    fc1_grad[0].finish()
-    fc1_grad[1].ring.forward()
+    mixed[...] = (row_all[my_rows, :].astype(F32) + branch.ring.total()).astype(BF16)
+    stores = []
+
+    def store(src, dst):
+        stores.append(pltpu.make_async_copy(src, dst, store_sems.at[len(stores)]))
+        stores[-1].start()
+
+    def store_grad(grad, out):
+        grad.finish()
+        cols = pl.ds(grad.lo, grad.units)
+        store(grad.out.at[:, cols], out.at[:, cols])
+
+    store(mixed, mixed_ref)
+    store_grad(fc2_grad[0], fc2_grad_ref)
+    store_grad(fc1_grad[0], fc1_grad_ref)
     total = add_finish(gain_z, adding)
-    gain_grad_ref[...] = (total / gain).reshape(width)
-    fc2_grad[1].finish()
-    fc1_grad[1].finish()
+    gain_out[...] = (total / gain).reshape(width)
+    store(gain_out, gain_grad_ref)
     for made in returned:
         made.wait_recv()
+    store(tgrad, tgrad_ref)
+    store_grad(fc2_grad[1], fc2_grad_ref)
+    store_grad(fc1_grad[1], fc1_grad_ref)
+    for made in stores:
+        made.wait()
     for made in started:
         made.wait_send()
     if len(started) != copies:
@@ -619,7 +688,7 @@
     )(*arrays)
 
 
-COPIES = 121
+COPIES = 130
 
 
 def local(tokens, norm_gain, fc1, fc2t, block_slot, out_grad):
@@ -647,11 +716,18 @@
             anywhere,
             anywhere,
         ],
-        out_specs=(vmem,) * 5,
+        out_specs=(anywhere,) * 5,
         scratch_shapes=[
             pltpu.VMEM((units, width), BF16),
             pltpu.VMEM((units, width), BF16),
             pltpu.VMEM(tokens.shape, BF16),
+            pltpu.VMEM((RING - 1, sz.block_rows, sz.cuts[1][1]), BF16),
+            pltpu.VMEM((RING - 1, sz.block_rows, sz.cuts[1][1]), BF16),
+            pltpu.VMEM((sz.own, width), BF16),
+            pltpu.VMEM(tokens.shape, BF16),
+            pltpu.VMEM((sz.owned, units), F32),
+            pltpu.VMEM((sz.owned, units), F32),
+            pltpu.VMEM((width,), F32),
             pltpu.VMEM((sz.rows, width), BF16),
             pltpu.VMEM((sz.own, 128), F32),
             pltpu.VMEM((sz.rows, width), BF16),
@@ -682,6 +758,7 @@
             pltpu.VMEM((RING, 1, width), F32),
             pltpu.VMEM((RING, 1, width), F32),
             pltpu.SemaphoreType.DMA((4,)),
+            pltpu.SemaphoreType.DMA((7,)),
             pltpu.SemaphoreType.DMA((COPIES,)),
             pltpu.SemaphoreType.DMA((COPIES,)),
         ],

time: 85.9 us -> 76.9 us (0.90)
  Pallas kernels: 85.1 us -> 76.1 us
    pallas_call x1, Pallas kernels: 82.5 us -> 73.5 us  [local(): pl.pallas_call(functools.partial(kernel, sz, COPIES), out_shape=(jax.Shap...]
where the time goes in v7:
time: 76.9 us; the launch traced here: 76.7 us
  Pallas kernels  76.1 us (99%)
    pallas_call x1, Pallas kernels, local(): pl.pallas_call(functools.partial(kernel, sz, COPIES), out_shape=(jax.Shap...  73.5 us
    pallas_call x1, Pallas kernels, hand_over(): pl.pallas_call(hand_over_kernel, out_shape=tuple((jax.ShapeDtypeStruct(a....  2.56 us

profile of v7, /device:TPU:0, one launch (start us, length us, event | category | flops | bytes accessed | tf_op | source)
XLA Modules:
  0.0 76.7 jit_solution(8378911377521672829)
XLA Ops:
  0.6 73.5 %mlp_block.1 = (bf16[32,3200]{1,0:T(8,128)(2,1)}, bf16[5,16,3200]{2,1,0:T(8,128)(2,1)}, f32[200,800]{1,0:T(8,128)}, f32[200,800]{1,0:T(8,128)}, f32[3200]{0:T(1024)}) custom-call(s32[80]{0:T(128)} %slot_ref.1, f32[3200]{0:T(1024)} %gain_ref.1, bf16[5,16,3200]{2,1,0:T(8,128)(2,1)} %tokens_hbm.1, bf16[800,3200]{1,0:T(8,128)(2,1)} %bitcast.4, ...), custom_call_target="tpu_custom_call" | custom-call | flops 7864320000 | bytes 10240000 | tf_op jit(solution)/shard_map/mlp_block/pallas_call | solution.py:702
  74.2 2.6 %hand_over.1 = (bf16[32,3200]{1,0:T(8,128)(2,1)}, bf16[5,16,3200]{2,1,0:T(8,128)(2,1)}, f32[200,800]{1,0:T(8,128)}, f32[200,800]{1,0:T(8,128)}, f32[3200]{0:T(1024)}) custom-call(bf16[32,3200]{1,0:T(8,128)(2,1)} %get-tuple-element.15.refs_0_, bf16[5,16,3200]{2,1,0:T(8,128)(2,1)} %get-tuple-element.16.refs_1_, f32[200,800]{1,0:T(8,128)} %get-tuple-element.17.refs_2_, ...), custom_call_target="tpu_custom_call" | custom-call | tf_op jit(solution)/shard_map/hand_over/pallas_call | solution.py:679

commit v8 on v7

--- a/solution.py
+++ b/solution.py
@@ -61,21 +61,16 @@
     fc1_hbm,
     fc2_hbm,
     grad_hbm,
-    mixed_ref,
-    tgrad_ref,
-    fc1_grad_ref,
-    fc2_grad_ref,
-    gain_grad_ref,
+    mixed,
+    tgrad,
+    fc1_out,
+    fc2_out,
+    gain_out,
     fc1_ref,
     fc2_ref,
     arrived,
     midway,
     midway_back,
-    mixed,
-    tgrad,
-    fc1_out,
-    fc2_out,
-    gain_out,
     row_all,
     inv_ref,
     grad_all,
@@ -106,7 +101,6 @@
     gain_y,
     gain_z,
     local_sems,
-    store_sems,
     send_sems,
     recv_sems,
 ):
@@ -169,8 +163,6 @@
     load_fc1 = pltpu.make_async_copy(fc1_hbm, fc1_ref, local_sems.at[3])
     load_grad.start()
     load_token.start()
-    load_fc2.start()
-    load_fc1.start()
 
     partners = [on_dp(k) for k in range(1, sz.homes)]
     partners += [on_dp(-k) for k in range(1, sz.homes)]
@@ -375,6 +367,8 @@
         last.append(send(tokens_hbm.at[j, :, cols1], arrived.at[j, :, cols1], on_dp(j)))
     load_grad.wait()
     grad_rows.start()
+    load_fc2.start()
+    load_fc1.start()
 
     def pick(s, j):
         home = (dp - j + RANKS) % RANKS
@@ -627,30 +621,14 @@
     fc1_grad[1].ring.forward()
     branch.ring.finish()
     mixed[...] = (row_all[my_rows, :].astype(F32) + branch.ring.total()).astype(BF16)
-    stores = []
-
-    def store(src, dst):
-        stores.append(pltpu.make_async_copy(src, dst, store_sems.at[len(stores)]))
-        stores[-1].start()
-
-    def store_grad(grad, out):
-        grad.finish()
-        cols = pl.ds(grad.lo, grad.units)
-        store(grad.out.at[:, cols], out.at[:, cols])
-
-    store(mixed, mixed_ref)
-    store_grad(fc2_grad[0], fc2_grad_ref)
-    store_grad(fc1_grad[0], fc1_grad_ref)
+    fc2_grad[0].finish()
+    fc1_grad[0].finish()
     total = add_finish(gain_z, adding)
     gain_out[...] = (total / gain).reshape(width)
-    store(gain_out, gain_grad_ref)
     for made in returned:
         made.wait_recv()
-    store(tgrad, tgrad_ref)
-    store_grad(fc2_grad[1], fc2_grad_ref)
-    store_grad(fc1_grad[1], fc1_grad_ref)
-    for made in stores:
-        made.wait()
+    fc2_grad[-1].finish()
+    fc1_grad[-1].finish()
     for made in started:
         made.wait_send()
     if len(started) != copies:
@@ -658,32 +636,27 @@
 
 
 def hand_over_kernel(*refs):
-    count = (len(refs) - 2) // 3
-    source, target, held = refs[:count], refs[count : 2 * count], refs[2 * count : 3 * count]
-    in_sems, out_sems = refs[-2:]
-    loads, stores = [], []
-    for i in range(count):
-        loads.append(pltpu.make_async_copy(source[i], held[i], in_sems.at[i]))
-        stores.append(pltpu.make_async_copy(held[i], target[i], out_sems.at[i]))
-    for one in loads:
+    count = len(refs) // 2
+    sems = refs[-1]
+    made = [
+        pltpu.make_async_copy(refs[i], refs[count + i], sems.at[i]) for i in range(count)
+    ]
+    for one in made:
         one.start()
-    for load, store in zip(loads, stores):
-        load.wait()
-        store.start()
-    for one in stores:
+    for one in made:
         one.wait()
 
 
 def hand_over(*arrays):
+    vmem = pl.BlockSpec(memory_space=pltpu.VMEM)
     anywhere = pl.BlockSpec(memory_space=pl.ANY)
     return pl.pallas_call(
         hand_over_kernel,
         out_shape=tuple(jax.ShapeDtypeStruct(a.shape, a.dtype) for a in arrays),
-        in_specs=[anywhere] * len(arrays),
+        in_specs=[vmem] * len(arrays),
         out_specs=(anywhere,) * len(arrays),
-        scratch_shapes=[pltpu.VMEM(a.shape, a.dtype) for a in arrays]
-        + [pltpu.SemaphoreType.DMA((len(arrays),))] * 2,
-        compiler_params=pltpu.CompilerParams(vmem_limit_bytes=60 * 1024 * 1024),
+        scratch_shapes=[pltpu.SemaphoreType.DMA((len(arrays),))],
+        compiler_params=pltpu.CompilerParams(vmem_limit_bytes=1024 * 1024),
         name="hand_over",
     )(*arrays)
 
@@ -702,11 +675,11 @@
     arrays = pl.pallas_call(
         functools.partial(kernel, sz, COPIES),
         out_shape=(
-            jax.ShapeDtypeStruct((sz.own, width), BF16),
-            jax.ShapeDtypeStruct(tokens.shape, BF16),
-            jax.ShapeDtypeStruct((sz.owned, units), F32),
-            jax.ShapeDtypeStruct((sz.owned, units), F32),
-            jax.ShapeDtypeStruct((width,), F32),
+            pltpu.VMEM((sz.own, width), BF16),
+            pltpu.VMEM(tokens.shape, BF16),
+            pltpu.VMEM((sz.owned, units), F32),
+            pltpu.VMEM((sz.owned, units), F32),
+            pltpu.VMEM((width,), F32),
         ),
         in_specs=[
             pl.BlockSpec(memory_space=pltpu.SMEM),
@@ -716,18 +689,13 @@
             anywhere,
             anywhere,
         ],
-        out_specs=(anywhere,) * 5,
+        out_specs=(vmem,) * 5,
         scratch_shapes=[
             pltpu.VMEM((units, width), BF16),
             pltpu.VMEM((units, width), BF16),
             pltpu.VMEM(tokens.shape, BF16),
             pltpu.VMEM((RING - 1, sz.block_rows, sz.cuts[1][1]), BF16),
             pltpu.VMEM((RING - 1, sz.block_rows, sz.cuts[1][1]), BF16),
-            pltpu.VMEM((sz.own, width), BF16),
-            pltpu.VMEM(tokens.shape, BF16),
-            pltpu.VMEM((sz.owned, units), F32),
-            pltpu.VMEM((sz.owned, units), F32),
-            pltpu.VMEM((width,), F32),
             pltpu.VMEM((sz.rows, width), BF16),
             pltpu.VMEM((sz.own, 128), F32),
             pltpu.VMEM((sz.rows, width), BF16),
@@ -758,7 +726,6 @@
             pltpu.VMEM((RING, 1, width), F32),
             pltpu.VMEM((RING, 1, width), F32),
             pltpu.SemaphoreType.DMA((4,)),
-            pltpu.SemaphoreType.DMA((7,)),
             pltpu.SemaphoreType.DMA((COPIES,)),
             pltpu.SemaphoreType.DMA((COPIES,)),
         ],

time: 76.9 us -> 74.9 us (0.974)
  Pallas kernels: 76.1 us -> 74.1 us
    pallas_call x1, Pallas kernels: 2.56 us -> 1.38 us  [hand_over(): pl.pallas_call(hand_over_kernel, out_shape=tuple((jax.ShapeDtypeStruct(a....]
    pallas_call x1, Pallas kernels: 73.5 us -> 72.7 us  [local(): pl.pallas_call(functools.partial(kernel, sz, COPIES), out_shape=(pltpu.VM...]
where the time goes in v8:
time: 74.9 us; the launch traced here: 74.7 us
  Pallas kernels  74.1 us (99%)
    pallas_call x1, Pallas kernels, local(): pl.pallas_call(functools.partial(kernel, sz, COPIES), out_shape=(pltpu.VM...  72.7 us

profile of v8, /device:TPU:0, one launch (start us, length us, event | category | flops | bytes accessed | tf_op | source)
XLA Modules:
  0.0 74.7 jit_solution(16172485314204344489)
XLA Ops:
  0.6 72.7 %mlp_block.1 = (bf16[32,3200]{1,0:T(8,128)(2,1)S(1)}, bf16[5,16,3200]{2,1,0:T(8,128)(2,1)S(1)}, f32[200,800]{1,0:T(8,128)S(1)}, f32[200,800]{1,0:T(8,128)S(1)}, f32[3200]{0:T(1024)S(1)}) custom-call(s32[80]{0:T(128)} %slot_ref.1, f32[3200]{0:T(1024)} %gain_ref.1, bf16[5,16,3200]{2,1,0:T(8,128)(2,1)} %tokens_hbm.1, bf16[800,3200]{1,0:T(8,128)(2,1)} %bitcast.4, ...), custom_call_target="tpu_custom_call" | custom-call | flops 7864320000 | bytes 10240000 | tf_op jit(solution)/shard_map/mlp_block/pallas_call | solution.py:675
  73.4 1.4 %hand_over.1 = (bf16[32,3200]{1,0:T(8,128)(2,1)}, bf16[5,16,3200]{2,1,0:T(8,128)(2,1)}, f32[200,800]{1,0:T(8,128)}, f32[200,800]{1,0:T(8,128)}, f32[3200]{0:T(1024)}) custom-call(bf16[32,3200]{1,0:T(8,128)(2,1)S(1)} %get-tuple-element.15.refs_0_, bf16[5,16,3200]{2,1,0:T(8,128)(2,1)S(1)} %get-tuple-element.16.refs_1_, ...), custom_call_target="tpu_custom_call" | custom-call | tf_op jit(solution)/shard_map/hand_over/pallas_call | solution.py:653

commit v9 on v8

--- a/solution.py
+++ b/solution.py
@@ -213,11 +213,11 @@
                 made.wait_recv()
 
     class RingGather:
-        def __init__(self, buf, lo, count, on_axis):
+        def __init__(self, buf, lo, count, on_axis, low):
             self.buf, self.on_axis = buf, on_axis
             self.whole = pl.ds(lo, count)
-            self.low = pl.ds(lo, count // 2)
-            self.high = pl.ds(lo + count // 2, count // 2)
+            self.low = pl.ds(lo, low)
+            self.high = pl.ds(lo + low, count - low)
 
         def start(self):
             buf, on_axis = self.buf, self.on_axis
@@ -308,8 +308,8 @@
             self.ring.start()
 
     class WeightGrad:
-        def __init__(self, index, p, slices, blocks, on_axis, owner_row, out):
-            self.index, self.p, self.out = index, p, out
+        def __init__(self, index, p, slices, blocks, on_axis, owner_row, out, mid):
+            self.index, self.p, self.out, self.mid = index, p, out, mid
             self.slices, self.blocks = slices, blocks
             self.lo, self.units = sz.parts[p]
             self.on_axis, self.owner_row = on_axis, owner_row
@@ -343,7 +343,7 @@
                 wg_out.at[index, p, :, :, pl.ds(0, units)],
                 wg_in.at[index, p, :, :, pl.ds(0, units)],
                 self.on_axis,
-                round_up(sz.owned_pad // 2, 16),
+                self.mid,
                 sz.owned_pad,
             )
             self.ring.start()
@@ -419,16 +419,18 @@
         inv = lax.rsqrt(jnp.mean(value * value, axis=-1, keepdims=True) + 1e-06)
         return value * inv, inv
 
-    def norm_range(first, stop):
-        @pl.loop(first // 16, stop // 16)
+    def norm_shard(slot, core):
+        @pl.loop(0, own // 16)
         def _(n):
-            rows = pl.ds(pl.multiple_of(n * 16, 16), 16)
+            place = sz.pair * slot + core * own + n * 16
+            rows = pl.ds(pl.multiple_of(place, 16), 16)
             unit, _ = normed_rows(rows)
             norm_all[rows, :] = (unit * gain).astype(BF16)
 
     unit_own, inv = normed_rows(my_rows)
     inv_ref[...] = jnp.broadcast_to(inv, inv_ref.shape)
     norm_own = (unit_own * gain).astype(BF16)
+    norm_all[my_rows, :] = norm_own
     for q in range(RING):
         norm_cut[q] = group_columns(norm_own, q)
     cut_sent = []
@@ -471,21 +473,26 @@
                 out[lo : lo + count, :] += part
 
     multiply_in(fc2_ref, *sz.parts[0], grad_all, hid_grad)
+    for slot in (1, 2):
+        norm_shard(slot, c)
     row_parts[1].last()
-    multiply_in(fc2_ref, *sz.parts[1], grad_all, hid_grad)
-    for one in row_parts:
-        one.wait(0, 3)
-    norm_range(0, 3 * sz.pair)
+    for slot in range(3):
+        for one in row_parts:
+            one.wait(slot, slot + 1)
+        norm_shard(slot, 1 - c)
+    norm_shard(3, c)
     for made in cut_sent:
         made.wait_recv()
     for one in row_parts:
         one.wait(3, 5)
+    norm_shard(3, 1 - c)
     cut_rows.start()
-    norm_range(3 * sz.pair, sz.rows)
     load_fc1.wait()
 
     hid_ring, pre_ring = [], []
     for lo, count in sz.parts:
+        if lo > 0:
+            multiply_in(fc2_ref, lo, count, grad_all, hid_grad)
         multiply_in(fc1_ref, lo, count, norm_all, pre_act)
 
         @pl.loop(0, count // 32)
@@ -497,8 +504,8 @@
             hid_g[0, rows, :] = (value * cdf).astype(BF16)
             pre_g[0, rows, :] = (hid_grad[rows, :] * slope).astype(BF16)
 
-        hid_ring.append(RingGather(hid_g, lo, count, on_y))
-        pre_ring.append(RingGather(pre_g, lo, count, on_z))
+        hid_ring.append(RingGather(hid_g, lo, count, on_y, count * 2 // 3 // 16 * 16))
+        pre_ring.append(RingGather(pre_g, lo, count, on_z, count // 2 // 16 * 16))
         hid_ring[-1].start()
         pre_ring[-1].start()
 
@@ -548,11 +555,13 @@
     def fc1_row(k):
         return ((y + STEP[k] + RING) % RING) * sz.owned
 
+    even = round_up(sz.owned_pad // 2, 16)
+    more = round_up(sz.owned_pad * 2 // 3, 16)
     fc2_grad = [
-        WeightGrad(0, p, grad_t, hid_g, on_z, fc2_row, fc2_out) for p in range(2)
+        WeightGrad(0, p, grad_t, hid_g, on_z, fc2_row, fc2_out, even) for p in range(2)
     ]
     fc1_grad = [
-        WeightGrad(1, p, norm_t, pre_g, on_y, fc1_row, fc1_out) for p in range(2)
+        WeightGrad(1, p, norm_t, pre_g, on_y, fc1_row, fc1_out, more) for p in range(2)
     ]
     hid_ring[0].finish()
     fc2_grad[0].multiply()
@@ -573,9 +582,10 @@
     fc1_grad[0].multiply()
     hid_ring[1].finish()
     fc2_grad[1].multiply()
-    fc2_grad[0].ring.forward()
     pre_ring[1].finish()
     fc1_grad[1].multiply()
+    fc2_grad[0].ring.forward()
+    fc1_grad[0].ring.forward()
     total = add_finish(gain_x, adding)
     adding = add_start(gain_y, y, on_y, total)
     back.ring.finish()
@@ -604,7 +614,8 @@
         else:
             returned.append(send(source, place, on_dp(-j)))
     branch.ring.forward()
-    fc1_grad[0].ring.forward()
+    fc2_grad[1].ring.forward()
+    fc1_grad[1].ring.forward()
     total = add_finish(gain_y, adding)
     adding = add_start(gain_z, z, on_z, total)
     for j in range(1, RING):
@@ -617,8 +628,6 @@
         def _():
             tgrad[j, :, lo1:] = midway_back[j - 1]
 
-    fc2_grad[1].ring.forward()
-    fc1_grad[1].ring.forward()
     branch.ring.finish()
     mixed[...] = (row_all[my_rows, :].astype(F32) + branch.ring.total()).astype(BF16)
     fc2_grad[0].finish()

time: 74.9 us -> 74.1 us (0.989)
  Pallas kernels: 74.1 us -> 73.3 us
    pallas_call x1, Pallas kernels: 72.7 us -> 71.9 us  [local(): pl.pallas_call(functools.partial(kernel, sz, COPIES), out_shape=(pltpu.VM...]
where the time goes in v9:
time: 74.1 us; the launch traced here: 73.9 us
  Pallas kernels  73.3 us (99%)
    pallas_call x1, Pallas kernels, local(): pl.pallas_call(functools.partial(kernel, sz, COPIES), out_shape=(pltpu.VM...  71.9 us

profile of v9, /device:TPU:0, one launch (start us, length us, event | category | flops | bytes accessed | tf_op | source)
XLA Modules:
  0.0 73.9 jit_solution(3255746357912962543)
XLA Ops:
  0.6 71.9 %mlp_block.1 = (bf16[32,3200]{1,0:T(8,128)(2,1)S(1)}, bf16[5,16,3200]{2,1,0:T(8,128)(2,1)S(1)}, f32[200,800]{1,0:T(8,128)S(1)}, f32[200,800]{1,0:T(8,128)S(1)}, f32[3200]{0:T(1024)S(1)}) custom-call(s32[80]{0:T(128)} %slot_ref.1, f32[3200]{0:T(1024)} %gain_ref.1, bf16[5,16,3200]{2,1,0:T(8,128)(2,1)} %tokens_hbm.1, bf16[800,3200]{1,0:T(8,128)(2,1)} %bitcast.4, ...), custom_call_target="tpu_custom_call" | custom-call | flops 7864320000 | bytes 10240000 | tf_op jit(solution)/shard_map/mlp_block/pallas_call | solution.py:684
  72.6 1.4 %hand_over.1 = (bf16[32,3200]{1,0:T(8,128)(2,1)}, bf16[5,16,3200]{2,1,0:T(8,128)(2,1)}, f32[200,800]{1,0:T(8,128)}, f32[200,800]{1,0:T(8,128)}, f32[3200]{0:T(1024)}) custom-call(bf16[32,3200]{1,0:T(8,128)(2,1)S(1)} %get-tuple-element.15.refs_0_, bf16[5,16,3200]{2,1,0:T(8,128)(2,1)S(1)} %get-tuple-element.16.refs_1_, ...), custom_call_target="tpu_custom_call" | custom-call | tf_op jit(solution)/shard_map/hand_over/pallas_call | solution.py:662

commit v10 on v9

--- a/solution.py
+++ b/solution.py
@@ -28,6 +28,34 @@
         if tiles % count == 0 and count * 128 <= limit:
             best = count
     return best * 128
+
+
+FOLD = 4
+
+
+def fold_rows(rows):
+    return round_up((rows + FOLD - 1) // FOLD, 16)
+
+
+def fold_lanes(value):
+    rows, units = value.shape
+    step = fold_rows(rows)
+    total = -(-rows // step)
+    if total * step > rows:
+        value = jnp.concatenate(
+            [value, jnp.zeros((total * step - rows, units), value.dtype)], axis=0
+        )
+    cuts = [value[step * k : step * (k + 1)] for k in range(total)]
+    if total * units < 128:
+        cuts.append(jnp.zeros((step, 128 - total * units), value.dtype))
+    return jnp.concatenate(cuts, axis=1)
+
+
+def unfold_lanes(value, rows, units):
+    step = value.shape[0]
+    total = -(-rows // step)
+    cuts = [value[:, units * k : units * (k + 1)] for k in range(total)]
+    return jnp.concatenate(cuts, axis=0)[:rows]
 
 
 class Sizes:
@@ -94,6 +122,8 @@
     wg_sum,
     wg_out,
     wg_in,
+    fold_out,
+    fold_in,
     back_out,
     input_grad,
     gain_sib,
@@ -237,43 +267,71 @@
             self.left2.wait_recv()
 
     class RingReduce:
-        def __init__(self, part, out, into, on_axis, mid, count):
+        def __init__(self, part, out, into, on_axis, mid, count, folds=None):
             self.part, self.out, self.into = part, out, into
-            self.on_axis, self.mid, self.count = on_axis, mid, count
+            self.on_axis, self.folds = on_axis, folds
+            self.ranges = ((0, mid), (mid, count - mid))
+
+        def put(self, slot, h, value):
+            first, count = self.ranges[h]
+            if self.folds is not None:
+                main, fold_out, _ = self.folds
+                folded = fold_lanes(value[:, main:])
+                fold_out[slot, h, 0 : folded.shape[0]] = folded.astype(BF16)
+                value = value[:, :main]
+            self.out[slot, pl.ds(first, count)] = value.astype(BF16)
+
+        def ship(self, slot, h, device):
+            first, count = self.ranges[h]
+            rows = pl.ds(first, count)
+            made = [send(self.out.at[slot, rows], self.into.at[slot, rows], device)]
+            if self.folds is not None:
+                main, fold_out, fold_in = self.folds
+                rows = pl.ds(0, fold_rows(count))
+                made.append(send(fold_out.at[slot, h, rows], fold_in.at[slot, h, rows], device))
+            return made
+
+        def get(self, slot, h):
+            first, count = self.ranges[h]
+            value = self.into[slot, pl.ds(first, count)].astype(F32)
+            if self.folds is not None:
+                main, _, fold_in = self.folds
+                folded = fold_in[slot, h, 0 : fold_rows(count)].astype(F32)
+                units = self.units - main
+                value = jnp.concatenate([value, unfold_lanes(folded, count, units)], axis=1)
+            return value
+
+        def own_part(self, k, h):
+            value = self.part(k, *self.ranges[h])
+            self.units = value.shape[1]
+            return value
 
         def start(self):
-            mid, rest = self.mid, self.count - self.mid
-            lo, hi = pl.ds(0, mid), pl.ds(mid, rest)
-            part, out, into, on_axis = self.part, self.out, self.into, self.on_axis
-            out[0, lo] = part(3, 0, mid).astype(BF16)
-            self.far_right = send(out.at[0, lo], into.at[0, lo], on_axis(1))
-            out[0, hi] = part(3, mid, rest).astype(BF16)
-            self.far_left = send(out.at[0, hi], into.at[0, hi], on_axis(-1))
-            out[1, hi] = part(2, mid, rest).astype(BF16)
-            self.near_right = send(out.at[1, hi], into.at[1, hi], on_axis(1))
-            out[2, lo] = part(1, 0, mid).astype(BF16)
-            self.near_left = send(out.at[2, lo], into.at[2, lo], on_axis(-1))
+            self.put(0, 0, self.own_part(3, 0))
+            self.far_right = self.ship(0, 0, self.on_axis(1))
+            self.put(0, 1, self.own_part(3, 1))
+            self.far_left = self.ship(0, 1, self.on_axis(-1))
+            self.put(1, 1, self.own_part(2, 1))
+            self.rest = self.ship(1, 1, self.on_axis(1))
+            self.put(2, 0, self.own_part(1, 0))
+            self.rest += self.ship(2, 0, self.on_axis(-1))
 
         def forward(self):
-            mid, rest = self.mid, self.count - self.mid
-            lo, hi = pl.ds(0, mid), pl.ds(mid, rest)
-            part, out, into, on_axis = self.part, self.out, self.into, self.on_axis
-            self.far_right.wait_recv()
-            out[1, lo] = (part(2, 0, mid) + into[0, lo].astype(F32)).astype(BF16)
-            self.sum_right = send(out.at[1, lo], into.at[1, lo], on_axis(1))
-            self.far_left.wait_recv()
-            out[2, hi] = (part(1, mid, rest) + into[0, hi].astype(F32)).astype(BF16)
-            self.sum_left = send(out.at[2, hi], into.at[2, hi], on_axis(-1))
+            for made in self.far_right:
+                made.wait_recv()
+            self.put(1, 0, self.own_part(2, 0) + self.get(0, 0))
+            self.rest += self.ship(1, 0, self.on_axis(1))
+            for made in self.far_left:
+                made.wait_recv()
+            self.put(2, 1, self.own_part(1, 1) + self.get(0, 1))
+            self.rest += self.ship(2, 1, self.on_axis(-1))
 
         def finish(self):
-            self.near_right.wait_recv()
-            self.near_left.wait_recv()
-            self.sum_right.wait_recv()
-            self.sum_left.wait_recv()
-
-        def total(self):
-            first = self.part(0, 0, self.count) + self.into[1].astype(F32)
-            return first + self.into[2].astype(F32)
+            for made in self.rest:
+                made.wait_recv()
+
+        def total(self, h):
+            return self.own_part(0, h) + self.get(1, h) + self.get(2, h)
 
     class RowReduce:
         def __init__(self, index):
@@ -338,19 +396,27 @@
                 place = pl.multiple_of(self.owner_row(k) + first, 8)
                 return wg_sum[index, p, pl.ds(place, count), 0:units]
 
+            main = units // 128 * 128
+            folds = None
+            if main < units:
+                folds = (main, fold_out.at[index], fold_in.at[index])
             self.ring = RingReduce(
                 part,
-                wg_out.at[index, p, :, :, pl.ds(0, units)],
-                wg_in.at[index, p, :, :, pl.ds(0, units)],
+                wg_out.at[index, p, :, :, pl.ds(0, main)],
+                wg_in.at[index, p, :, :, pl.ds(0, main)],
                 self.on_axis,
                 self.mid,
                 sz.owned_pad,
+                folds,
             )
             self.ring.start()
 
         def finish(self):
             self.ring.finish()
-            self.out[:, self.lo : self.lo + self.units] = self.ring.total()[: sz.owned]
+            for h, (first, count) in enumerate(self.ring.ranges):
+                count = min(count, sz.owned - first)
+                cols = slice(self.lo, self.lo + self.units)
+                self.out[first : first + count, cols] = self.ring.total(h)[:count]
 
     grad_rows = RowGather(lambda rows: grad_all.at[rows])
     cut_rows = RowGather(lambda rows: norm_sl.at[pl.ds(1, RING - 1), rows])
@@ -590,7 +656,7 @@
     adding = add_start(gain_y, y, on_y, total)
     back.ring.finish()
 
-    normed_grad = back.ring.total()
+    normed_grad = jnp.concatenate([back.ring.total(0), back.ring.total(1)], axis=0)
     unit = row_all[my_rows, :].astype(F32) * inv_ref[:, :1]
     scaled = normed_grad * gain
     inner = scaled - unit * jnp.mean(scaled * unit, axis=-1, keepdims=True)
@@ -629,7 +695,8 @@
             tgrad[j, :, lo1:] = midway_back[j - 1]
 
     branch.ring.finish()
-    mixed[...] = (row_all[my_rows, :].astype(F32) + branch.ring.total()).astype(BF16)
+    branch_sum = jnp.concatenate([branch.ring.total(0), branch.ring.total(1)], axis=0)
+    mixed[...] = (row_all[my_rows, :].astype(F32) + branch_sum).astype(BF16)
     fc2_grad[0].finish()
     fc1_grad[0].finish()
     total = add_finish(gain_z, adding)
@@ -670,7 +737,7 @@
     )(*arrays)
 
 
-COPIES = 130
+COPIES = 142
 
 
 def local(tokens, norm_gain, fc1, fc2t, block_slot, out_grad):
@@ -680,7 +747,8 @@
     anywhere = pl.BlockSpec(memory_space=pl.ANY)
     slices = (RING, sz.rows, sz.group_pad)
     slices_t = (RING, sz.group_pad, sz.rows)
-    pieces = (2, 2, 3, sz.owned_pad, sz.part_max)
+    pieces = (2, 2, 3, sz.owned_pad, sz.part_max // 128 * 128)
+    folds = (2, 3, 2, fold_rows(sz.owned_pad), 128)
     arrays = pl.pallas_call(
         functools.partial(kernel, sz, COPIES),
         out_shape=(
@@ -728,6 +796,8 @@
             pltpu.VMEM((2, 2, sz.sum_rows, sz.part_max), F32),
             pltpu.VMEM(pieces, BF16),
             pltpu.VMEM(pieces, BF16),
+            pltpu.VMEM(folds, BF16),
+            pltpu.VMEM(folds, BF16),
             pltpu.VMEM((sz.homes - 1, sz.block_rows, width), BF16),
             pltpu.VMEM((sz.own, width), F32),
             pltpu.VMEM((2, 1, width), F32),

time: 74.1 us -> 73.4 us (level)
  no operation moved by 1% of the time
where the time goes in v10:
time: 73.4 us; the launch traced here: 73.3 us
  Pallas kernels  72.6 us (99%)
    pallas_call x1, Pallas kernels, local(): pl.pallas_call(functools.partial(kernel, sz, COPIES), out_shape=(pltpu.VM...  71.2 us

profile of v10, /device:TPU:0, one launch (start us, length us, event | category | flops | bytes accessed | tf_op | source)
XLA Modules:
  0.0 73.3 jit_solution(10745612213820731592)
XLA Ops:
  0.6 71.2 %mlp_block.1 = (bf16[32,3200]{1,0:T(8,128)(2,1)S(1)}, bf16[5,16,3200]{2,1,0:T(8,128)(2,1)S(1)}, f32[200,800]{1,0:T(8,128)S(1)}, f32[200,800]{1,0:T(8,128)S(1)}, f32[3200]{0:T(1024)S(1)}) custom-call(s32[80]{0:T(128)} %slot_ref.1, f32[3200]{0:T(1024)} %gain_ref.1, bf16[5,16,3200]{2,1,0:T(8,128)(2,1)} %tokens_hbm.1, bf16[800,3200]{1,0:T(8,128)(2,1)} %bitcast.4, ...), custom_call_target="tpu_custom_call" | custom-call | flops 7864320000 | bytes 10240000 | tf_op jit(solution)/shard_map/mlp_block/pallas_call | solution.py:752
  71.9 1.4 %hand_over.1 = (bf16[32,3200]{1,0:T(8,128)(2,1)}, bf16[5,16,3200]{2,1,0:T(8,128)(2,1)}, f32[200,800]{1,0:T(8,128)}, f32[200,800]{1,0:T(8,128)}, f32[3200]{0:T(1024)}) custom-call(bf16[32,3200]{1,0:T(8,128)(2,1)S(1)} %get-tuple-element.15.refs_0_, bf16[5,16,3200]{2,1,0:T(8,128)(2,1)S(1)} %get-tuple-element.16.refs_1_, ...), custom_call_target="tpu_custom_call" | custom-call | tf_op jit(solution)/shard_map/hand_over/pallas_call | solution.py:729

commit v11 on v10

--- a/solution.py
+++ b/solution.py
@@ -523,20 +523,9 @@
     load_fc2.wait()
 
     def multiply_in(lhs, lo, count, rows, out):
-        @pl.loop(0, width // sz.chunk)
-        def _(n):
-            cols = pl.ds(pl.multiple_of(n * sz.chunk, sz.chunk), sz.chunk)
-            part = lax.dot_general(
-                lhs[lo : lo + count, cols], rows[:, cols], ROW_DIMS, preferred_element_type=F32
-            )
-
-            @pl.when(n == 0)
-            def _():
-                out[lo : lo + count, :] = part
-
-            @pl.when(n > 0)
-            def _():
-                out[lo : lo + count, :] += part
+        out[lo : lo + count, :] = lax.dot_general(
+            lhs[lo : lo + count, :], rows[...], ROW_DIMS, preferred_element_type=F32
+        )
 
     multiply_in(fc2_ref, *sz.parts[0], grad_all, hid_grad)
     for slot in (1, 2):
@@ -632,7 +621,6 @@
     hid_ring[0].finish()
     fc2_grad[0].multiply()
     back.ring.forward()
-    branch.start()
     gain_pair.wait_recv()
     adding = add_start(gain_x, x, on_x, gain_sib[0] + gain_sib[1])
     cut_rows.wait(0, 5)
@@ -652,6 +640,7 @@
     fc1_grad[1].multiply()
     fc2_grad[0].ring.forward()
     fc1_grad[0].ring.forward()
+    branch.start()
     total = add_finish(gain_x, adding)
     adding = add_start(gain_y, y, on_y, total)
     back.ring.finish()
@@ -673,13 +662,14 @@
             tgrad[0] = total
             continue
         back_out[j - 1] = total
+        if j < RING:
+            source = back_out.at[j - 1, :, cols1]
+            via.append(send(source, midway_back.at[j - 1], on_z(-j)))
+    for j in range(1, sz.homes):
         source, place = back_out.at[j - 1], tgrad.at[j]
         if j < RING:
-            via.append(send(source.at[:, cols1], midway_back.at[j - 1], on_z(-j)))
-            returned.append(send(source.at[:, cols0], place.at[:, cols0], on_dp(-j)))
-        else:
-            returned.append(send(source, place, on_dp(-j)))
-    branch.ring.forward()
+            source, place = source.at[:, cols0], place.at[:, cols0]
+        returned.append(send(source, place, on_dp(-j)))
     fc2_grad[1].ring.forward()
     fc1_grad[1].ring.forward()
     total = add_finish(gain_y, adding)
@@ -694,6 +684,7 @@
         def _():
             tgrad[j, :, lo1:] = midway_back[j - 1]
 
+    branch.ring.forward()
     branch.ring.finish()
     branch_sum = jnp.concatenate([branch.ring.total(0), branch.ring.total(1)], axis=0)
     mixed[...] = (row_all[my_rows, :].astype(F32) + branch_sum).astype(BF16)

time: 73.4 us -> 73.3 us (level)
  no operation moved by 1% of the time
where the time goes in v11:
time: 73.3 us; the launch traced here: 73.1 us
  Pallas kernels  72.5 us (99%)
    pallas_call x1, Pallas kernels, local(): pl.pallas_call(functools.partial(kernel, sz, COPIES), out_shape=(pltpu.VM...  71.1 us

profile of v11, /device:TPU:0, one launch (start us, length us, event | category | flops | bytes accessed | tf_op | source)
XLA Modules:
  0.0 73.1 jit_solution(16342310001946066512)
XLA Ops:
  0.6 71.1 %mlp_block.1 = (bf16[32,3200]{1,0:T(8,128)(2,1)S(1)}, bf16[5,16,3200]{2,1,0:T(8,128)(2,1)S(1)}, f32[200,800]{1,0:T(8,128)S(1)}, f32[200,800]{1,0:T(8,128)S(1)}, f32[3200]{0:T(1024)S(1)}) custom-call(s32[80]{0:T(128)} %slot_ref.1, f32[3200]{0:T(1024)} %gain_ref.1, bf16[5,16,3200]{2,1,0:T(8,128)(2,1)} %tokens_hbm.1, bf16[800,3200]{1,0:T(8,128)(2,1)} %bitcast.4, ...), custom_call_target="tpu_custom_call" | custom-call | flops 7864320000 | bytes 10240000 | tf_op jit(solution)/shard_map/mlp_block/pallas_call | solution.py:743
  71.8 1.4 %hand_over.1 = (bf16[32,3200]{1,0:T(8,128)(2,1)}, bf16[5,16,3200]{2,1,0:T(8,128)(2,1)}, f32[200,800]{1,0:T(8,128)}, f32[200,800]{1,0:T(8,128)}, f32[3200]{0:T(1024)}) custom-call(bf16[32,3200]{1,0:T(8,128)(2,1)S(1)} %get-tuple-element.15.refs_0_, bf16[5,16,3200]{2,1,0:T(8,128)(2,1)S(1)} %get-tuple-element.16.refs_1_, ...), custom_call_target="tpu_custom_call" | custom-call | tf_op jit(solution)/shard_map/hand_over/pallas_call | solution.py:720
